TPU v7x, 32 devices: a whole 2x2x4 slice. The times are simulated.
32 devices in a mesh: shard: 2 (over x), ctx: 4 (over y, core), tp: 4 (over z).
Axes of the slice: x: 2, y: 2, z: 4, core: 2. Of those that a mesh axis runs over, the one named last changes fastest.
Arguments:
- tokens_in: bfloat16 [8, 1024, 768], P('shard', 'ctx'), may hold values from -6 to 6
- qkv_weight: bfloat16 [3, 768, 768], P(None, ('shard', 'ctx'), 'tp'), may hold values from -0.21875 to 0.21875
- qv_bias: bfloat16 [2, 768], P(None, 'tp'), may hold values from -3 to 3
- out_weight: bfloat16 [768, 768], P('tp', ('shard', 'ctx')), may hold values from -0.875 to 0.875
- geglu_weight: bfloat16 [2, 768, 3072], P(None, ('shard', 'ctx'), 'tp'), may hold values from -0.21875 to 0.21875
- geglu_bias: bfloat16 [2, 3072], P(None, 'tp'), may hold values from -3 to 3
- down_weight: bfloat16 [3072, 768], P('tp', ('shard', 'ctx')), may hold values from -0.15625 to 0.15625
- norm_gains: bfloat16 [2, 768], P(None, ('shard', 'ctx')), may hold values from 0.099609375 to 1.8984375
- norm_biases: bfloat16 [2, 768], P(None, ('shard', 'ctx')), may hold values from -2 to 2
- out_biases: bfloat16 [2, 768], P(None, ('shard', 'ctx')), may hold values from -2 to 2
- doc_lengths: int32 [8, 8], P('shard'), may hold values from 1 to 1017, as said below
- cotangent: bfloat16 [8, 1024, 768], P('shard', 'ctx'), may hold values from -6 to 6
Outputs:
- layer_out: bfloat16 [8, 1024, 768], P('shard', 'ctx')
- input_grad: float32 [8, 1024, 768], P('shard', 'ctx')
- grad_qkv: float32 [3, 768, 768], P(None, ('shard', 'ctx'), 'tp')
- grad_qv_bias: float32 [2, 768], P(None, 'tp')
- grad_out_weight: float32 [768, 768], P('tp', ('shard', 'ctx'))
- grad_geglu_weight: float32 [2, 768, 3072], P(None, ('shard', 'ctx'), 'tp')
- grad_geglu_bias: float32 [2, 3072], P(None, 'tp')
- grad_down_weight: float32 [3072, 768], P('tp', ('shard', 'ctx'))
- grad_norm_gains: float32 [2, 768], P(None, ('shard', 'ctx'))
- grad_norm_biases: float32 [2, 768], P(None, ('shard', 'ctx'))
- grad_out_biases: float32 [2, 768], P(None, ('shard', 'ctx'))
Inputs may be any that keep to these rules, and one draw needn't show every extreme that they name: `doc_lengths`: each row holds 8 positive document lengths that sum to 1024; documents fill the sequence in order.
All inputs are finite; a program needn't handle non-finite values.
Results may differ from a plain program's by a relative error of at most 0.015.
Values may be sent and summed in bfloat16 or wider, within the bound.
A program may use at most 256 MiB of HBM per device.

v0:
```python
import math

import jax
import jax.numpy as jnp
from jax import lax
from jax.sharding import PartitionSpec as P

H = 12
DH = 64


def alibi_slopes(head_count):

    def power_slopes(head_total):
        first_slope = 2.0 ** (-8.0 / head_total)
        return [first_slope ** (counter + 1) for counter in range(head_total)]

    nearest = 2 ** int(math.floor(math.log2(head_count)))
    slope_list = power_slopes(nearest)
    slope_list = slope_list + power_slopes(2 * nearest)[0::2][: head_count - nearest]
    return slope_list


def layer_norm(values, gain_vector, shift_vector):
    center = values - jnp.mean(values, axis=-1, keepdims=True)
    spread = jnp.mean(center * center, axis=-1, keepdims=True)
    return center * lax.rsqrt(spread + 1e-12) * gain_vector + shift_vector


def norm_param_grads(values, upstream):
    center = values - jnp.mean(values, axis=-1, keepdims=True)
    spread = jnp.mean(center * center, axis=-1, keepdims=True)
    scaled = center * lax.rsqrt(spread + 1e-12)
    return (jnp.sum(upstream * scaled, axis=0), jnp.sum(upstream, axis=0))


def exact_gelu(values):
    return jax.nn.gelu(values, approximate=False)


def segment_ids(lengths, positions):
    doc_ends = jnp.cumsum(lengths, axis=-1)
    return jnp.sum((positions[None, :, None] >= doc_ends[:, None, :]).astype(jnp.int32), axis=-1)


def plain_dot(left, right):
    return jnp.dot(left, right, preferred_element_type=jnp.float32)


def contract_rows(left, right):
    return lax.dot_general(
        left, right, (((0,), (0,)), ((), ())), preferred_element_type=jnp.float32
    )


def times_transposed(left, right):
    return lax.dot_general(
        left, right, (((1,), (1,)), ((), ())), preferred_element_type=jnp.float32
    )


def on_device(
    tokens_in,
    qkv_weight,
    qv_bias,
    out_weight,
    geglu_weight,
    geglu_bias,
    down_weight,
    norm_gains,
    norm_biases,
    out_biases,
    doc_lengths,
    cotangent,
):
    seq_count, row_count, model_width = tokens_in.shape
    total_rows = seq_count * row_count
    token_rows = tokens_in.reshape(total_rows, model_width)
    local_heads = qv_bias.shape[1] // DH
    score_scale = 1.0 / math.sqrt(DH)
    share = total_rows // lax.axis_size("tp")
    share_start = lax.axis_index("tp") * share

    def rows_of(values):
        return lax.dynamic_slice_in_dim(values, share_start, share, 0)

    gathered = (
        lax.all_gather(qkv_weight, ("shard", "ctx"), axis=1, tiled=True),
        lax.all_gather(out_weight, ("shard", "ctx"), axis=1, tiled=True),
        lax.all_gather(geglu_weight, ("shard", "ctx"), axis=1, tiled=True),
        lax.all_gather(down_weight, ("shard", "ctx"), axis=1, tiled=True),
        lax.all_gather(norm_gains, ("shard", "ctx"), axis=1, tiled=True),
        lax.all_gather(norm_biases, ("shard", "ctx"), axis=1, tiled=True),
        lax.all_gather(out_biases, ("shard", "ctx"), axis=1, tiled=True),
    )
    w_qkv, w_out, w_geglu, w_down, gain_rows, shift_rows, bias_rows = gathered
    first_gain = gain_rows[0].astype(jnp.float32)
    first_shift = shift_rows[0].astype(jnp.float32)
    second_gain = gain_rows[1].astype(jnp.float32)
    second_shift = shift_rows[1].astype(jnp.float32)
    queries = (plain_dot(token_rows, w_qkv[0]) + qv_bias[0].astype(jnp.float32)).astype(
        jnp.bfloat16
    )
    key_rows = plain_dot(token_rows, w_qkv[1]).astype(jnp.bfloat16)
    value_rows = (plain_dot(token_rows, w_qkv[2]) + qv_bias[1].astype(jnp.float32)).astype(
        jnp.bfloat16
    )
    all_keys, all_values = (
        lax.all_gather(key_rows.reshape(seq_count, row_count, -1), "ctx", axis=1, tiled=True),
        lax.all_gather(value_rows.reshape(seq_count, row_count, -1), "ctx", axis=1, tiled=True),
    )
    length = all_keys.shape[1]
    query_heads = queries.reshape(seq_count, row_count, local_heads, DH)
    key_heads = all_keys.reshape(seq_count, length, local_heads, DH)
    value_heads = all_values.reshape(seq_count, length, local_heads, DH)
    query_pos = lax.axis_index("ctx") * row_count + jnp.arange(row_count, dtype=jnp.int32)
    key_pos = jnp.arange(length, dtype=jnp.int32)
    same_doc = (
        segment_ids(doc_lengths, query_pos)[:, :, None]
        == segment_ids(doc_lengths, key_pos)[:, None, :]
    )
    distance = jnp.abs(query_pos[:, None] - key_pos[None, :]).astype(jnp.float32)
    slope_table = jnp.asarray(alibi_slopes(H), jnp.float32)
    head_slopes = lax.dynamic_slice_in_dim(
        slope_table, lax.axis_index("tp") * local_heads, local_heads
    )

    def scores_of():
        raw_scores = (
            jnp.einsum(
                "sqhd,skhd->shqk", query_heads, key_heads, preferred_element_type=jnp.float32
            )
            * score_scale
        )
        raw_scores = raw_scores - head_slopes[None, :, None, None] * distance[None, None]
        return jnp.where(same_doc[:, None], raw_scores, -1e30)

    scores = scores_of()
    row_max = jnp.max(scores, axis=-1, keepdims=True)
    powered = jnp.exp(scores - row_max)
    row_total = jnp.sum(powered, axis=-1, keepdims=True)
    probs_low = (powered / row_total).astype(jnp.bfloat16)
    log_total = row_max + jnp.log(row_total)
    mixed_heads = jnp.einsum(
        "shqk,skhd->sqhd", probs_low, value_heads, preferred_element_type=jnp.float32
    )
    mixed_heads = mixed_heads.reshape(total_rows, local_heads * DH).astype(jnp.bfloat16)
    attended = lax.psum(plain_dot(mixed_heads, w_out), "tp") + bias_rows[0].astype(jnp.float32)
    residual_one = token_rows.astype(jnp.float32) + attended
    normed = layer_norm(residual_one, first_gain, first_shift)
    normed_low = normed.astype(jnp.bfloat16)
    residual_one_share = rows_of(residual_one)
    gate_pre = plain_dot(normed_low, w_geglu[0]) + geglu_bias[0].astype(jnp.float32)
    upward = plain_dot(normed_low, w_geglu[1]) + geglu_bias[1].astype(jnp.float32)
    gate_act, gelu_pull = jax.vjp(exact_gelu, gate_pre)
    hidden = (gate_act * upward).astype(jnp.bfloat16)
    upstream = cotangent.reshape(total_rows, model_width).astype(jnp.float32)
    upstream_share = rows_of(upstream)
    branch = lax.psum(plain_dot(hidden, w_down), "tp") + bias_rows[1].astype(jnp.float32)
    residual_two = normed + branch
    output_low = layer_norm(residual_two, second_gain, second_shift).astype(jnp.bfloat16)
    second_vals, second_pull = jax.vjp(layer_norm, residual_two, second_gain, second_shift)
    d_res2 = second_pull(upstream)[0]
    d_branch = d_res2.astype(jnp.bfloat16)
    residual_two_share = rows_of(residual_two)
    d_gain2, d_shift2 = norm_param_grads(residual_two_share, upstream_share)
    d_bias_down = jnp.sum(d_branch.astype(jnp.float32), axis=0)
    grad_down = contract_rows(hidden, d_branch)
    d_hidden = times_transposed(d_branch, w_down)
    d_gate = gelu_pull(d_hidden * upward)[0].astype(jnp.bfloat16)
    d_up = (d_hidden * gate_act).astype(jnp.bfloat16)
    d_geglu_bias = jnp.stack(
        [jnp.sum(d_gate.astype(jnp.float32), axis=0), jnp.sum(d_up.astype(jnp.float32), axis=0)]
    )
    grad_geglu = jnp.stack([contract_rows(normed_low, d_gate), contract_rows(normed_low, d_up)])
    d_normed_part = times_transposed(d_gate, w_geglu[0]) + times_transposed(d_up, w_geglu[1])
    d_normed = lax.psum(d_normed_part, "tp") + d_res2
    first_vals, first_pull = jax.vjp(layer_norm, residual_one, first_gain, first_shift)
    d_res1 = first_pull(d_normed)[0]
    d_normed_share = rows_of(d_normed)
    d_gain1, d_shift1 = norm_param_grads(residual_one_share, d_normed_share)
    d_attended = d_res1.astype(jnp.bfloat16)
    d_bias_attn = jnp.sum(d_attended.astype(jnp.float32), axis=0)
    grad_out = contract_rows(mixed_heads, d_attended)
    d_mixed = times_transposed(d_attended, w_out).astype(jnp.bfloat16)
    probs = jnp.exp(scores_of() - log_total)
    probs_back = probs.astype(jnp.bfloat16)
    d_mixed_heads = d_mixed.reshape(seq_count, row_count, local_heads, DH)
    d_probs = jnp.einsum(
        "sqhd,skhd->shqk", d_mixed_heads, value_heads, preferred_element_type=jnp.float32
    )
    d_values_part = jnp.einsum(
        "shqk,sqhd->skhd", probs_back, d_mixed_heads, preferred_element_type=jnp.float32
    )
    row_dot = jnp.sum(probs * d_probs, axis=-1, keepdims=True)
    d_scores = (probs * (d_probs - row_dot)).astype(jnp.bfloat16)
    d_queries = (
        jnp.einsum("shqk,skhd->sqhd", d_scores, key_heads, preferred_element_type=jnp.float32)
        * score_scale
    )
    d_queries = d_queries.reshape(total_rows, local_heads * DH).astype(jnp.bfloat16)
    d_keys_part = (
        jnp.einsum("shqk,sqhd->skhd", d_scores, query_heads, preferred_element_type=jnp.float32)
        * score_scale
    )
    d_keys_sum, d_values_sum = (
        lax.psum_scatter(
            d_keys_part.reshape(seq_count, length, -1), "ctx", scatter_dimension=1, tiled=True
        ),
        lax.psum_scatter(
            d_values_part.reshape(seq_count, length, -1), "ctx", scatter_dimension=1, tiled=True
        ),
    )
    d_keys = d_keys_sum.reshape(total_rows, -1).astype(jnp.bfloat16)
    d_values = d_values_sum.reshape(total_rows, -1).astype(jnp.bfloat16)
    d_qv_bias = jnp.stack(
        [
            jnp.sum(d_queries.astype(jnp.float32), axis=0),
            jnp.sum(d_values.astype(jnp.float32), axis=0),
        ]
    )
    grad_qkv_part = jnp.stack(
        [
            contract_rows(token_rows, d_queries),
            contract_rows(token_rows, d_keys),
            contract_rows(token_rows, d_values),
        ]
    )
    d_input_part = (
        times_transposed(d_queries, w_qkv[0])
        + times_transposed(d_keys, w_qkv[1])
        + times_transposed(d_values, w_qkv[2])
    )
    grad_gains_part = jnp.stack([d_gain1, d_gain2])
    grad_shifts_part = jnp.stack([d_shift1, d_shift2])
    input_sum, grad_gains, grad_shifts = (
        lax.psum(d_input_part.astype(jnp.bfloat16), "tp").astype(jnp.float32),
        lax.psum(grad_gains_part.astype(jnp.bfloat16), "tp").astype(jnp.float32),
        lax.psum(grad_shifts_part.astype(jnp.bfloat16), "tp").astype(jnp.float32),
    )
    input_grad = input_sum + d_res1
    grad_biases = jnp.stack([d_bias_attn, d_bias_down])
    owners = lax.axis_size(("shard", "ctx"))
    qv_spread = jnp.broadcast_to(d_qv_bias[:, None, :], (2, owners, d_qv_bias.shape[1]))
    geglu_spread = jnp.broadcast_to(d_geglu_bias[:, None, :], (2, owners, d_geglu_bias.shape[1]))
    summed = (
        lax.psum_scatter(grad_qkv_part, ("shard", "ctx"), scatter_dimension=1, tiled=True),
        lax.psum_scatter(grad_out, ("shard", "ctx"), scatter_dimension=1, tiled=True),
        lax.psum_scatter(grad_geglu, ("shard", "ctx"), scatter_dimension=1, tiled=True),
        lax.psum_scatter(grad_down, ("shard", "ctx"), scatter_dimension=1, tiled=True),
        lax.psum_scatter(grad_gains, ("shard", "ctx"), scatter_dimension=1, tiled=True),
        lax.psum_scatter(grad_shifts, ("shard", "ctx"), scatter_dimension=1, tiled=True),
        lax.psum_scatter(grad_biases, ("shard", "ctx"), scatter_dimension=1, tiled=True),
        lax.psum_scatter(qv_spread, ("shard", "ctx"), scatter_dimension=1, tiled=True),
        lax.psum_scatter(geglu_spread, ("shard", "ctx"), scatter_dimension=1, tiled=True),
    )
    return (
        output_low.reshape(seq_count, row_count, model_width),
        input_grad.reshape(seq_count, row_count, model_width),
        summed[0],
        summed[7][:, 0, :],
        summed[1],
        summed[2],
        summed[8][:, 0, :],
        summed[3],
        summed[4],
        summed[5],
        summed[6],
    )


def solution(mesh):
    in_specs = (
        P("shard", "ctx", None),
        P(None, ("shard", "ctx"), "tp"),
        P(None, "tp"),
        P("tp", ("shard", "ctx")),
        P(None, ("shard", "ctx"), "tp"),
        P(None, "tp"),
        P("tp", ("shard", "ctx")),
        P(None, ("shard", "ctx")),
        P(None, ("shard", "ctx")),
        P(None, ("shard", "ctx")),
        P("shard", None),
        P("shard", "ctx", None),
    )
    out_specs = (
        P("shard", "ctx", None),
        P("shard", "ctx", None),
        P(None, ("shard", "ctx"), "tp"),
        P(None, "tp"),
        P("tp", ("shard", "ctx")),
        P(None, ("shard", "ctx"), "tp"),
        P(None, "tp"),
        P("tp", ("shard", "ctx")),
        P(None, ("shard", "ctx")),
        P(None, ("shard", "ctx")),
        P(None, ("shard", "ctx")),
    )
    return jax.shard_map(
        on_device, mesh=mesh, in_specs=in_specs, out_specs=out_specs, check_vma=False
    )
```

profile of v0, /device:TPU:0, one launch (start us, length us, event | category | flops | bytes accessed | tf_op | source)
XLA Modules:
  0.0 1201.5 jit_solution(12250533347392013152)
XLA Ops:
  8.1 13.3 %all_gather.27 = bf16[3,768,192]{2,1,0:T(8,128)(2,1)S(1)} all-gather(bf16[3,96,192]{2,1,0:T(8,128)(2,1)} %param.14), channel_id=1, replica_groups=mesh['shard'=2,'ctx'=4,'tp'=4] {'shard','ctx'}, dimensions={1}, use_global_device_ids=true | all-gather | bytes 995328 | tf_op jit(solution)/shard_map/all_gather | solution.py:88
  21.4 2.5 convolution_convert_fusion.1
  27.8 11.1 all_gather.30
  48.0 3.3 fusion.44
  51.3 4.6 copy-done
  55.9 2.6 fusion
  58.5 9.8 all-gather.8.cloned.1.call-done
  70.2 6.6 fusion.18
  81.5 8.7 all-gather.1
  90.3 7.8 all-gather.2
  98.2 9.0 all-gather
  109.2 92.3 %all-reduce.9.cloned.1.call-done = f32[1024,768]{1,0:T(8,128)} async-done(((f32[1024,768]{1,0:T(8,128)}), f32[1024,768]{1,0:T(8,128)}) %all-reduce.9.cloned.1.call-update) | async-done | bytes 3145744 | tf_op jit(solution)/shard_map/psum | solution.py:148
  201.5 2.8 fusion.43
  207.2 3.3 fusion.20
  212.1 9.4 multiply_convert_fusion.2
  221.5 4.9 fusion.46
  227.0 119.6 %all-reduce.11.cloned.1.call-done = f32[1024,768]{1,0:T(8,128)} async-done(((f32[1024,768]{1,0:T(8,128)}), f32[1024,768]{1,0:T(8,128)}) %all-reduce.11.cloned.1.call-update) | async-done | bytes 3145744 | tf_op jit(solution)/shard_map/psum | solution.py:159
  346.7 3.0 fusion.41
  350.9 2.7 fusion.40
  357.1 4.1 convert_reduce_fusion.2
  362.9 3.1 convolution_add_fusion
  367.0 119.3 %all-reduce.13.cloned.1.call-done = f32[1024,768]{1,0:T(8,128)} async-done(((f32[1024,768]{1,0:T(8,128)}), f32[1024,768]{1,0:T(8,128)}) %all-reduce.13.cloned.1.call-update) | async-done | bytes 3145744 | tf_op jit(solution)/shard_map/psum | solution.py:177
  486.3 3.9 multiply_reduce_fusion.1
  498.5 6.7 multiply_reduce_fusion
  505.2 6.2 multiply_convert_fusion
  511.5 3.4 convolution_multiply_fusion
  515.1 48.6 %copy.81 = f32[4,1024,192]{0,2,1:T(8,128)} copy(f32[4,1024,192]{1,2,0:T(8,128)} %bitcast.180) | data formatting | bytes 6291456
  563.7 84.3 %reshape.228 = f32[1024,768]{1,0:T(8,128)} reshape(f32[1024,192,4]{2,1,0:T(8,128)} %bitcast.43) | data formatting | bytes 6291456
  648.3 8.6 fusion.2
  656.9 48.6 %copy.83 = f32[4,1024,192]{0,2,1:T(8,128)} copy(f32[4,1024,192]{1,2,0:T(8,128)} %bitcast.179) | data formatting | bytes 6291456
  705.5 84.3 %reshape.230 = f32[1024,768]{1,0:T(8,128)} reshape(f32[1024,192,4]{2,1,0:T(8,128)} %bitcast.46) | data formatting | bytes 6291456
  794.2 9.3 all-reduce.3
  804.6 6.6 convert_reduce_fusion.5
  818.1 29.2 %reshape.229 = bf16[256,192,4]{2,1,0:T(8,128)(2,1)} reshape(f32[256,768]{1,0:T(8,128)} %reduce-scatter.28.cloned.1.call-done) | data formatting | bytes 1179648
  847.2 12.2 %copy.82 = bf16[4,256,192]{1,0,2:T(4,128)(2,1)S(1)} copy(bf16[4,256,192]{0,2,1:T(8,128)(2,1)} %bitcast.175) | data formatting | bytes 786432
  859.5 29.2 %reshape.231 = bf16[256,192,4]{2,1,0:T(8,128)(2,1)} reshape(f32[256,768]{1,0:T(8,128)} %reduce-scatter.30.cloned.1.call-done) | data formatting | bytes 1179648
  888.7 12.2 %copy.84 = bf16[4,256,192]{1,0,2:T(4,128)(2,1)S(1)} copy(bf16[4,256,192]{0,2,1:T(8,128)(2,1)} %bitcast.176) | data formatting | bytes 786432
  908.4 3.0 copy.85
  911.4 2.8 reshape.232
  914.3 4.9 fusion.47
  929.9 7.5 reduce-scatter.40.cloned.1.call-done
  938.8 36.7 %reduce-scatter.34.cloned.1.call-done = f32[96,192]{1,0:T(8,128)} async-done(((f32[768,192]{1,0:T(8,128)}), f32[96,192]{1,0:T(8,128)}) %reduce-scatter.34.cloned.1.call-update) | async-done | bytes 73744
  979.0 24.4 %all-reduce.2 = (f32[2,8,192]{2,0,1:T(2,128)S(1)}, f32[2,8,768]{2,0,1:T(2,128)S(1)}) all-reduce(f32[2,8,192]{2,0,1:T(2,128)S(1)} %broadcast_in_dim.34, f32[2,8,768]{2,0,1:T(2,128)S(1)} %broadcast_in_dim.35), channel_id=5, replica_groups=mesh['shard'=2,'ctx'=4,'tp'=4] {'shard','ctx'}, use_global_device_ids=true, to_apply=%region_23.24.clone | all-reduce | flops 15360 | bytes 122880
  1005.9 41.1 %all-reduce.15.cloned.1.call-done = bf16[1024,768]{1,0:T(8,128)(2,1)} async-done(((bf16[1024,768]{1,0:T(8,128)(2,1)}), bf16[1024,768]{1,0:T(8,128)(2,1)}) %all-reduce.15.cloned.1.call-update) | async-done | bytes 1572880 | tf_op jit(solution)/shard_map/psum | solution.py:237
  1046.9 3.4 convert_add_fusion
  1050.4 39.3 %reduce-scatter.32.cloned.1.call-done = f32[96,576]{1,0:T(8,128)} async-done(((f32[768,576]{1,0:T(8,128)}), f32[96,576]{1,0:T(8,128)}) %reduce-scatter.32.cloned.1.call-update) | async-done | bytes 221200
  1091.6 44.8 %reduce-scatter.26.cloned.1.call-done = f32[768,96]{0,1:T(8,128)} async-done(((f32[768,768]{0,1:T(8,128)}), f32[768,96]{0,1:T(8,128)}) %reduce-scatter.26.cloned.1.call-update) | async-done | bytes 294928 | tf_op jit(solution)/shard_map/reduce_scatter | solution.py:250
  1136.4 57.8 %reduce-scatter.24.cloned.1.call-done = f32[2,96,768]{2,1,0:T(8,128)} async-done(((f32[2,768,768]{2,1,0:T(8,128)}), f32[2,96,768]{2,1,0:T(8,128)}) %reduce-scatter.24.cloned.1.call-update) | async-done | bytes 589840 | tf_op jit(solution)/shard_map/reduce_scatter | solution.py:249
  (283 shorter events, 81.8 us)
Async XLA Ops:
  8.0 17.1 %copy-start.2 = (bf16[4,256,768]{2,1,0:T(8,128)(2,1)S(1)}, bf16[4,256,768]{2,1,0:T(8,128)(2,1)}, u32[]{:S(2)}) copy-start(bf16[4,256,768]{2,1,0:T(8,128)(2,1)} %param.13) | copy-start | bytes 4718596
  8.0 17.0 %copy-start.59 = (bf16[2,192]{1,0:T(2,128)(2,1)S(1)}, bf16[2,192]{1,0:T(2,128)(2,1)}, u32[]{:S(2)}) copy-start(bf16[2,192]{1,0:T(2,128)(2,1)} %param.15) | copy-start | bytes 2308
  8.0 38.0 %all-gather.10.cloned.1.call-start = ((), (), s32[]{:S(2)}) async-start(), calls=%async_computation.10 | async-start | bytes 1966080 | tf_op jit(solution)/shard_map/all_gather | solution.py:109
  21.4 17.6 %copy-start.15 = (bf16[3,768,192]{2,1,0:T(8,128)(2,1)}, bf16[3,768,192]{2,1,0:T(8,128)(2,1)S(1)}, u32[]{:S(2)}) copy-start(bf16[3,768,192]{2,1,0:T(8,128)(2,1)S(1)} %all_gather.27) | copy-start | bytes 2654212
  21.4 6.0 copy-start.60
  21.4 6.3 copy-start.40
  25.0 43.3 %all-gather.8.cloned.1.call-start = ((), (), s32[]{:S(2)}) async-start(), calls=%async_computation.9 | async-start | bytes 1966080 | tf_op jit(solution)/shard_map/all_gather | solution.py:110
  26.8 174.7 %all-reduce.9.cloned.1.call-start = ((), (), s32[]{:S(2)}) async-start(), calls=%async_computation.11 | async-start | bytes 6291456 | tf_op jit(solution)/shard_map/psum | solution.py:148
  27.6 11.4 copy-start.47
  39.9 8.1 copy-start.19
  51.3 18.9 %copy-start.34 = (f32[4,3,256]{2,1,0:T(4,128)}, f32[4,3,256]{2,1,0:T(4,128)S(1)}, u32[]{:S(2)}) copy-start(f32[4,3,256]{2,1,0:T(4,128)S(1)} %get-tuple-element.100) | copy-start | bytes 36868
  58.5 18.3 %copy-start.39 = (f32[4,3,256]{2,1,0:T(4,128)}, f32[4,3,256]{2,1,0:T(4,128)S(1)}, u32[]{:S(2)}) copy-start(f32[4,3,256]{2,1,0:T(4,128)S(1)} %fusion) | copy-start | bytes 36868
  70.2 6.6 copy-start.18
  70.2 7.7 copy-start.21
  77.9 12.4 %copy-start.62 = (bf16[2,96]{1,0:T(2,128)(2,1)S(1)}, bf16[2,96]{1,0:T(2,128)(2,1)}, u32[]{:S(2)}) copy-start(bf16[2,96]{1,0:T(2,128)(2,1)} %param.21) | copy-start | bytes 1156
  77.9 20.3 %copy-start.63 = (bf16[2,96]{1,0:T(2,128)(2,1)S(1)}, bf16[2,96]{1,0:T(2,128)(2,1)}, u32[]{:S(2)}) copy-start(bf16[2,96]{1,0:T(2,128)(2,1)} %param.22) | copy-start | bytes 1156
  78.0 30.7 %copy-start.51 = (bf16[2,768]{1,0:T(2,128)(2,1)S(1)}, bf16[2,768]{1,0:T(2,128)(2,1)}, u32[]{:S(2)}) copy-start(bf16[2,768]{1,0:T(2,128)(2,1)} %param.18) | copy-start | bytes 9220
  80.3 126.9 %all-gather.12.cloned.1.call-start = ((), (), s32[]{:S(2)}) async-start(), calls=%async_computation.12 | async-start | bytes 2654208 | tf_op jit(solution)/shard_map/all_gather | solution.py:90
  80.9 140.7 %all-gather.14.cloned.1.call-start = ((), (), s32[]{:S(2)}) async-start(), calls=%async_computation.13 | async-start | bytes 1327104 | tf_op jit(solution)/shard_map/all_gather | solution.py:91
  81.5 265.2 %all-reduce.11.cloned.1.call-start = ((), (), s32[]{:S(2)}) async-start(), calls=%async_computation.14 | async-start | bytes 6291456 | tf_op jit(solution)/shard_map/psum | solution.py:159
  108.6 238.0 %copy-start.35 = (f32[768]{0:T(1024)}, f32[768]{0:T(1024)S(1)}, u32[]{:S(2)}) copy-start(f32[768]{0:T(1024)S(1)} %get-tuple-element.62) | copy-start | bytes 9220
  204.4 142.3 %copy-start.32 = (f32[1024]{0:T(1024)}, f32[1024]{0:T(1024)S(1)}, u32[]{:S(2)}) copy-start(f32[1024]{0:T(1024)S(1)} %broadcast_multiply_fusion.2) | copy-start | bytes 12292
  205.5 141.2 %copy-start.37 = (f32[1024]{0:T(1024)}, f32[1024]{0:T(1024)S(1)}, u32[]{:S(2)}) copy-start(f32[1024]{0:T(1024)S(1)} %fusion.31) | copy-start | bytes 12292
  207.2 5.0 copy-start.30
  207.2 5.0 copy-start.53
  226.4 259.9 %all-reduce.13.cloned.1.call-start = ((), (), s32[]{:S(2)}) async-start(), calls=%async_computation.15 | async-start | bytes 6291456 | tf_op jit(solution)/shard_map/psum | solution.py:177
  350.8 5.3 copy-start.69
  350.9 5.3 copy-start.70
  356.1 5.1 copy-start.27
  366.1 452.0 %reduce-scatter.28.cloned.1.call-start = ((), (), s32[]{:S(2)}) async-start(), calls=%async_computation.19 | async-start | bytes 3932160
  505.2 6.3 copy-start.20
  648.0 211.5 %reduce-scatter.30.cloned.1.call-start = ((), (), s32[]{:S(2)}) async-start(), calls=%async_computation.20 | async-start | bytes 3932160
  789.9 137.1 %reduce-scatter.36.cloned.1.call-start = ((), (), s32[]{:S(2)}) async-start(), calls=%async_computation.23 | async-start | bytes 442368
  804.5 7.6 copy-start.49
  804.5 8.8 copy-start.12
  804.5 8.8 copy-start.24
  804.5 123.9 %reduce-scatter.38.cloned.1.call-start = ((), (), s32[]{:S(2)}) async-start(), calls=%async_computation.24 | async-start | bytes 442368
  812.1 125.3 %reduce-scatter.40.cloned.1.call-start = ((), (), s32[]{:S(2)}) async-start(), calls=%async_computation.25 | async-start | bytes 442368
  813.2 162.4 %reduce-scatter.34.cloned.1.call-start = ((), (), s32[]{:S(2)}) async-start(), calls=%async_computation.22 | async-start | bytes 884736
  815.3 32.0 %copy-start.22 = (bf16[24,8,4,256]{3,1,2,0:T(8,128)(2,1)}, bf16[24,8,4,256]{3,1,2,0:T(8,128)(2,1)S(1)}, u32[]{:S(2)}) copy-start(bf16[24,8,4,256]{3,1,2,0:T(8,128)(2,1)S(1)} %copy.99) | copy-start | bytes 1179652
  815.3 231.7 %all-reduce.15.cloned.1.call-start = ((), (), s32[]{:S(2)}) async-start(), calls=%async_computation.16 | async-start | bytes 3145728 | tf_op jit(solution)/shard_map/psum | solution.py:237
  904.6 185.1 %reduce-scatter.32.cloned.1.call-start = ((), (), s32[]{:S(2)}) async-start(), calls=%async_computation.21 | async-start | bytes 2211840
  914.3 5.3 copy-start.26
  914.3 5.3 copy-start.29
  914.3 222.1 %reduce-scatter.26.cloned.1.call-start = ((), (), s32[]{:S(2)}) async-start(), calls=%async_computation.18 | async-start | bytes 2654208 | tf_op jit(solution)/shard_map/reduce_scatter | solution.py:250
  919.3 274.9 %reduce-scatter.24.cloned.1.call-start = ((), (), s32[]{:S(2)}) async-start(), calls=%async_computation.17 | async-start | bytes 5308416 | tf_op jit(solution)/shard_map/reduce_scatter | solution.py:249
  924.9 122.1 %copy-start.7 = (f32[1024,768]{1,0:T(8,128)S(1)}, f32[1024,768]{1,0:T(8,128)}, u32[]{:S(2)}) copy-start(f32[1024,768]{1,0:T(8,128)} %copy-done.6) | copy-start | bytes 9437188
  924.9 122.1 %copy-start.42 = (f32[1024]{0:T(1024)S(1)}, f32[1024]{0:T(1024)}, u32[]{:S(2)}) copy-start(f32[1024]{0:T(1024)} %copy-done.41) | copy-start | bytes 12292
  (40 other events, 102.8 us)
Sparse Core Ops, SparseCore 0:
  25.1 20.8 all-gather.9
  48.2 20.0 all-gather.7
  80.4 121.0 all-reduce.8
  226.5 120.0 all-reduce.10
  366.2 120.0 all-reduce.12
  648.2 36.9 reduce-scatter.27
  790.0 36.7 reduce-scatter.29
  829.8 33.8 reduce-scatter.35
  866.7 33.8 reduce-scatter.37
  903.5 33.8 reduce-scatter.39
  940.6 34.9 reduce-scatter.33
  977.8 69.0 all-reduce.14
  1050.3 39.3 reduce-scatter.31
  1093.9 42.4 reduce-scatter.25
  1140.2 53.8 reduce-scatter.23
Sparse Core Ops, SparseCore 1:
  82.7 28.8 all-gather.11
  113.3 23.9 all-gather.13
where the time goes:
time: 1210 us; the launch traced here: 1200 us
  waiting for transfers between devices  571 us (47%)
  local copies, waits for them, and re-layouts  394 us (33%)
  matrix products  85.5 us (7%)
  blocking collectives  83.8 us (7%)
  other arithmetic  48.1 us (4%)
  between operations  16.7 us (1%)
    unnamed x170, local copies, waits for them, and re-layouts  382 us
    psum x1, waiting for transfers between devices, on_device(): lax.psum(plain_dot(hidden, w_down), 'tp') + bias_rows[1].astype(jnp.float32)  120 us
    psum x1, waiting for transfers between devices, on_device(): d_normed = lax.psum(d_normed_part, 'tp') + d_res2  119 us
    psum x1, waiting for transfers between devices, on_device(): lax.psum(plain_dot(mixed_heads, w_out), 'tp')  92.3 us
    unnamed x24, waiting for transfers between devices  84.9 us
    reduce_scatter x1, waiting for transfers between devices, on_device(): lax.psum_scatter(grad_geglu, ('shard', 'ctx'), scatter_dimension=1, tiled...  57.8 us
    reduce_scatter x1, waiting for transfers between devices, on_device(): lax.psum_scatter(grad_down, ('shard', 'ctx'), scatter_dimension=1, tiled=...  44.8 us
    psum x1, waiting for transfers between devices, on_device(): lax.psum(d_input_part.astype(jnp.bfloat16), 'tp').astype(jnp.float32)  41.1 us
  transfers between devices with their start and end apart: 17, of which 11 were waited for; matrix products, arithmetic and copies ran while one was open for 27% of the time, Pallas kernels for 0%

commit v1 on v0

v1 whole, which is shorter than its diff:
```python
import functools
import math

import jax
import jax.numpy as jnp
from jax import lax
from jax.experimental import pallas as pl
from jax.experimental.pallas import tpu as pltpu
from jax.sharding import PartitionSpec as P

H = 12
DH = 64
F32 = jnp.float32
BF16 = jnp.bfloat16
MESH = pl.DeviceIdType.MESH
NCH = 2
TILE = 32
MB = 1 << 20


def alibi_slopes(head_count):
    def power_slopes(head_total):
        first_slope = 2.0 ** (-8.0 / head_total)
        return [first_slope ** (counter + 1) for counter in range(head_total)]

    nearest = 2 ** int(math.floor(math.log2(head_count)))
    slope_list = power_slopes(nearest)
    return slope_list + power_slopes(2 * nearest)[0::2][: head_count - nearest]


def dot(left, right):
    return jnp.dot(left, right, preferred_element_type=F32)


def dot_nt(left, right):
    return lax.dot_general(left, right, (((1,), (1,)), ((), ())), preferred_element_type=F32)


def dot_tn(left, right):
    return lax.dot_general(left, right, (((0,), (0,)), ((), ())), preferred_element_type=F32)


def vmem(count):
    return [pl.BlockSpec(memory_space=pltpu.VMEM)] * count


def attention_forward(
    heads, lengths, slopes, xs, w, bias, mixed, probs, q_out, k_out, v_out, far
):
    length = xs.shape[0]
    step = 256
    cols = heads * DH
    mine = lax.axis_index("ctx") * heads

    def project(r, carry):
        rows = pl.ds(pl.multiple_of(r * step, step), step)
        x_rows = xs[rows, :]
        for part, out in enumerate((q_out, k_out, v_out)):
            y = dot(x_rows, w[:, part * cols : (part + 1) * cols])
            if part != 1:
                y = y + bias[part // 2 : part // 2 + 1, :]
            y = y.astype(BF16)
            if part == 0:
                y = y * BF16(1.0 / math.sqrt(DH))
            for i in range(heads):
                out[i, rows, :] = y[:, i * DH : (i + 1) * DH]
        return carry

    lax.fori_loop(0, length // step, project, 0)

    def segments(pos):
        seg = jnp.zeros(pos.shape, jnp.int32)
        end = 0
        for k in range(lengths.shape[1]):
            end = end + lengths[0, k]
            seg = seg + (pos >= end).astype(jnp.int32)
        return seg

    key_pos = lax.broadcasted_iota(jnp.int32, (1, length), 1)
    key_seg = segments(key_pos)

    def attend(r, carry):
        start = pl.multiple_of(r * step, step)
        rows = pl.ds(start, step)
        pos = start + lax.broadcasted_iota(jnp.int32, (step, 1), 0)
        same = segments(pos) == key_seg
        far[...] = jnp.where(same, jnp.abs(pos - key_pos).astype(F32), 1e33)
        for i in range(heads):
            s = dot_nt(q_out[i, rows, :], k_out[i]) - slopes[0, mine + i] * far[...]
            p = jnp.exp(s - jnp.max(s, axis=-1, keepdims=True))
            p = (p * (1.0 / jnp.sum(p, axis=-1, keepdims=True))).astype(BF16)
            probs[i, rows, :] = p
            mixed[rows, i * DH : (i + 1) * DH] = dot(p, v_out[i]).astype(BF16)
        return carry

    lax.fori_loop(0, length // step, attend, 0)


def attention_backward(
    heads, dmixed, mixed, probs, q, k, v, xs, w, grad_w, d_in, bias_grad, dqkv, dk_acc, dv_acc
):
    length = xs.shape[0]
    step = 256
    cols = heads * DH
    dk_acc[...] = jnp.zeros_like(dk_acc)
    dv_acc[...] = jnp.zeros_like(dv_acc)

    def rows_back(r, carry):
        rows = pl.ds(pl.multiple_of(r * step, step), step)
        for i in range(heads):
            own = slice(i * DH, (i + 1) * DH)
            d_out = dmixed[rows, own]
            row_dot = jnp.sum(
                d_out.astype(F32) * mixed[rows, own].astype(F32), axis=-1, keepdims=True
            )
            p = probs[i, rows, :]
            dp = dot_nt(d_out, v[i])
            ds = (p.astype(F32) * (dp - row_dot)).astype(BF16)
            dqkv[rows, own] = (dot(ds, k[i]) * (1.0 / math.sqrt(DH))).astype(BF16)
            dk_acc[i] += dot_tn(q[i, rows, :], ds)
            dv_acc[i] += dot_tn(d_out, p)
        return carry

    lax.fori_loop(0, length // step, rows_back, 0)
    for i in range(heads):
        dqkv[:, cols + i * DH : cols + (i + 1) * DH] = dk_acc[i].T.astype(BF16)
        dqkv[:, 2 * cols + i * DH : 2 * cols + (i + 1) * DH] = dv_acc[i].T.astype(BF16)

    def finish(r, total):
        rows = pl.ds(pl.multiple_of(r * step, step), step)
        d = dqkv[rows, :]
        d_in[rows, :] = dot_nt(d, w[:, : 3 * cols]).astype(BF16)
        return total + jnp.sum(d.astype(F32), axis=0, keepdims=True)

    bias_grad[...] = lax.fori_loop(
        0, length // step, finish, jnp.zeros((1, 3 * cols), F32)
    )
    for part in range(3):
        own = slice(part * cols, (part + 1) * cols)
        grad_w[:, own] = dot_tn(xs[...], dqkv[:, own]).astype(BF16)


def middle(
    x, cot, mixed, w, vec,
    lout, dres1, grads, gout, dmixed, small,
    w_out, full, act, pull, hid, dgt, dup,
    snd_r, snd_o, snd_y, rcv_r, rcv_o, rcv_y,
    own, yacc, fa, fb, normed, zh1, r1, dres2, acc, bsum, tiny,
    ags_y, agr_y, ags_c, agr_c, ags_f, agr_f,
    rss_r, rsr_r, rss_o, rsr_o, rss_y, rsr_y, tiny_s, tiny_r,
):
    rows_own = x.shape[0]
    width = x.shape[1]
    cr = rows_own // NCH
    c = lax.axis_index("ctx")
    flip = 1 - 2 * (c % 2)
    sib = c + flip
    ynb = (c + 2) % 4
    dia = ynb + flip

    barrier = pltpu.get_barrier_semaphore()
    for peer in (sib, ynb):
        pl.semaphore_signal(barrier, inc=1, device_id={"ctx": peer}, device_id_type=MESH)
    pl.semaphore_wait(barrier, 2)

    started = []

    def remote(src, dst, send, recv, peer):
        return pltpu.make_async_remote_copy(
            src_ref=src, dst_ref=dst, send_sem=send, recv_sem=recv,
            device_id={"ctx": peer}, device_id_type=MESH,
        )

    def chunk(k):
        return pl.ds(k * cr, cr)

    ag_y, ag_c, ag_f, rs_r, rs_o, rs_y = ({} for _ in range(6))

    def start(table, key, copy):
        copy.start()
        table[key] = copy
        started.append(copy)

    def gather_start(o, k):
        piece = full.at[o, c, chunk(k)]
        start(ag_y, (o, k), remote(piece, piece, ags_y.at[o, k], agr_y.at[o, k], ynb))
        start(ag_c, (o, k), remote(piece, piece, ags_c.at[o, k], agr_c.at[o, k], sib))

    def forward(o, k):
        ag_y[o, k].wait_recv()
        piece = full.at[o, ynb, chunk(k)]
        start(ag_f, (o, k), remote(piece, piece, ags_f.at[o, k], agr_f.at[o, k], sib))

    def send_relay(o, k):
        start(rs_r, (o, k), remote(
            snd_r.at[o, chunk(k)], rcv_r.at[o, chunk(k)], rss_r.at[o, k], rsr_r.at[o, k], sib))

    def send_own(o, k):
        start(rs_o, (o, k), remote(
            snd_o.at[o, chunk(k)], rcv_o.at[o, chunk(k)], rss_o.at[o, k], rsr_o.at[o, k], sib))

    def relay(o, k):
        rs_r[o, k].wait_recv()
        snd_y[o, chunk(k), :] = (yacc[chunk(k), :] + rcv_r[o, chunk(k), :].astype(F32)).astype(BF16)
        start(rs_y, (o, k), remote(
            snd_y.at[o, chunk(k)], rcv_y.at[o, chunk(k)], rss_y.at[o, k], rsr_y.at[o, k], ynb))

    def arrived(o, k):
        rs_o[o, k].wait_recv()
        rs_y[o, k].wait_recv()

    def tiles(first, count, body):
        def step(t, carry):
            body(pl.ds(pl.multiple_of(first + t * TILE, TILE), TILE))
            return carry
        lax.fori_loop(0, count // TILE, step, 0)

    def summed(o, rows):
        return own[rows, :] + rcv_o[o, rows, :].astype(F32) + rcv_y[o, rows, :].astype(F32)

    def fold(values):
        return jnp.sum(values.reshape(TILE // 8, 8, width), axis=0)

    acc[...] = jnp.zeros_like(acc)
    bsum[...] = jnp.zeros_like(bsum)
    w_out[...] = w[0, :, 3 * mixed.shape[2] : 4 * mixed.shape[2]]

    def project(b, r0, n):
        return dot_nt(mixed[b, pl.ds(r0, n), :], w_out[...])

    for k in range(NCH):
        snd_r[0, chunk(k), :] = project(dia, k * cr, cr).astype(BF16)
        send_relay(0, k)
        yacc[chunk(k), :] = project(ynb, k * cr, cr)
        if k:
            relay(0, k - 1)
    relay(0, NCH - 1)
    for k in range(NCH):
        snd_o[0, chunk(k), :] = project(sib, k * cr, cr).astype(BF16)
        send_own(0, k)
    own[...] = project(c, 0, rows_own)

    def norm_one(rows):
        res = x[rows, :].astype(F32) + summed(0, rows) + vec[4:5, :]
        center = res - jnp.mean(res, axis=-1, keepdims=True)
        r = lax.rsqrt(jnp.mean(center * center, axis=-1, keepdims=True) + 1e-12)
        zh = center * r
        out = zh * vec[0:1, :] + vec[2:3, :]
        zh1[rows, :] = zh
        r1[rows, :] = r
        normed[rows, :] = out
        full[0, c, rows, :] = out.astype(BF16)

    for k in range(NCH):
        arrived(0, k)
        tiles(k * cr, cr, norm_one)
        gather_start(0, k)

    def mlp_forward(b, r0, n):
        rows_in = full[0, b, pl.ds(r0, n), :]
        fa[pl.ds(0, n), :] = dot(rows_in, w[1])
        fb[pl.ds(0, n), :] = dot(rows_in, w[2])

        def units(rows):
            g = fa[rows, :] + vec[6:7, :]
            u = fb[rows, :] + vec[7:8, :]
            phi = 0.5 * (1.0 + lax.erf(g * (1.0 / math.sqrt(2.0))))
            gelu = g * phi
            slope = phi + g * jnp.exp(-0.5 * g * g) * (1.0 / math.sqrt(2.0 * math.pi))
            out = pl.ds(pl.multiple_of(r0 + rows.start, TILE), TILE)
            act[b, out, :] = gelu.astype(BF16)
            pull[b, out, :] = (u * slope).astype(BF16)
            hid[b, out, :] = (gelu * u).astype(BF16)

        tiles(0, n, units)
        return dot_nt(hid[b, pl.ds(r0, n), :], w[3])

    def mlp_backward(b, r0, n):
        fa[pl.ds(0, n), :] = dot(full[1, b, pl.ds(r0, n), :], w[3])

        def units(rows):
            dh = fa[rows, :]
            out = pl.ds(pl.multiple_of(r0 + rows.start, TILE), TILE)
            dg = (dh * pull[b, out, :].astype(F32)).astype(BF16)
            du = (dh * act[b, out, :].astype(F32)).astype(BF16)
            dgt[b, out, :] = dg
            dup[b, out, :] = du
            bsum[0] += fold(dg.astype(F32))
            bsum[1] += fold(du.astype(F32))

        tiles(0, n, units)
        return dot_nt(dgt[b, pl.ds(r0, n), :], w[1]) + dot_nt(dup[b, pl.ds(r0, n), :], w[2])

    def exchange(o, piece):
        own[...] = piece(c, 0, rows_own)
        for k in range(NCH):
            ag_c[o - 1, k].wait_recv()
        snd_o[o] = piece(sib, 0, rows_own).astype(BF16)
        for k in range(NCH):
            send_own(o, k)
        for k in range(NCH):
            forward(o - 1, k)
            yacc[chunk(k), :] = piece(ynb, k * cr, cr)
            ag_f[o - 1, k].wait_recv()
            snd_r[o, chunk(k), :] = piece(dia, k * cr, cr).astype(BF16)
            send_relay(o, k)
            if k:
                relay(o, k - 1)
        relay(o, NCH - 1)

    exchange(1, mlp_forward)

    def norm_two(rows):
        res = normed[rows, :] + (summed(1, rows) + vec[5:6, :])
        center = res - jnp.mean(res, axis=-1, keepdims=True)
        r = lax.rsqrt(jnp.mean(center * center, axis=-1, keepdims=True) + 1e-12)
        zh = center * r
        lout[rows, :] = (zh * vec[1:2, :] + vec[3:4, :]).astype(BF16)
        up = cot[rows, :].astype(F32)
        t = up * vec[1:2, :]
        d = r * (t - jnp.mean(t, axis=-1, keepdims=True)
                 - zh * jnp.mean(t * zh, axis=-1, keepdims=True))
        dres2[rows, :] = d
        low = d.astype(BF16)
        full[1, c, rows, :] = low
        acc[1] += fold(up * zh)
        acc[3] += fold(up)
        acc[5] += fold(low.astype(F32))

    for k in range(NCH):
        arrived(1, k)
        tiles(k * cr, cr, norm_two)
        gather_start(1, k)

    exchange(2, mlp_backward)

    def flat(ref):
        return ref[...].reshape(4 * rows_own, ref.shape[-1])

    hid_all = flat(hid)
    d_all = full[1].reshape(4 * rows_own, width)
    grads[2] = dot_tn(d_all, hid_all).astype(BF16)
    n_all = full[0].reshape(4 * rows_own, width)
    grads[0] = dot_tn(n_all, flat(dgt)).astype(BF16)
    grads[1] = dot_tn(n_all, flat(dup)).astype(BF16)

    def norm_back(rows):
        dn = summed(2, rows) + dres2[rows, :]
        zh = zh1[rows, :]
        t = dn * vec[0:1, :]
        d = r1[rows, :] * (t - jnp.mean(t, axis=-1, keepdims=True)
                           - zh * jnp.mean(t * zh, axis=-1, keepdims=True))
        dres1[rows, :] = d
        low = d.astype(BF16)
        full[2, c, rows, :] = low
        acc[0] += fold(dn * zh)
        acc[2] += fold(dn)
        acc[4] += fold(low.astype(F32))

    for k in range(NCH):
        arrived(2, k)
        tiles(k * cr, cr, norm_back)
        gather_start(2, k)

    for i in range(6):
        tiny[0, i : i + 1, :] = jnp.sum(acc[i], axis=0, keepdims=True)
    for i in range(2):
        small[6 + i : 7 + i, :] = jnp.sum(bsum[i], axis=0, keepdims=True)
    tiny_copies = []
    for step, peer in enumerate((sib, ynb)):
        copy = remote(tiny.at[2 * step], tiny.at[2 * step + 1], tiny_s.at[step], tiny_r.at[step], peer)
        copy.start()
        started.append(copy)
        tiny_copies.append(copy)
        if step == 0:
            def unproject(b, r0, n):
                return dot(full[2, b, pl.ds(r0, n), :], w_out[...]).astype(BF16)
            dmixed[c] = unproject(c, 0, rows_own)
            for k in range(NCH):
                ag_c[2, k].wait_recv()
            dmixed[sib] = unproject(sib, 0, rows_own)
        copy.wait_recv()
        total = tiny[2 * step] + tiny[2 * step + 1]
        if step == 0:
            tiny[2] = total
        else:
            small[0:6, :] = total[0:6, :]
    for k in range(NCH):
        forward(2, k)
        dmixed[ynb, chunk(k), :] = unproject(ynb, k * cr, cr)
    for k in range(NCH):
        ag_f[2, k].wait_recv()
        dmixed[dia, chunk(k), :] = unproject(dia, k * cr, cr)
    gout[...] = dot_tn(full[2].reshape(4 * rows_own, width), flat(mixed)).astype(BF16)
    for copy in started:
        copy.wait_send()


def sds(shape, dtype):
    return jax.ShapeDtypeStruct(shape, dtype)


def smem():
    return pl.BlockSpec(memory_space=pltpu.SMEM)


def on_device(
    tokens_in, qkv_weight, qv_bias, out_weight, geglu_weight, geglu_bias, down_weight,
    norm_gains, norm_biases, out_biases, doc_lengths, cotangent,
):
    seqs, rows, width = tokens_in.shape
    group = lax.axis_size("ctx")
    tp = lax.axis_size("tp")
    shards = lax.axis_size("shard")
    z = lax.axis_index("tp")
    c = lax.axis_index("ctx")
    assert group == 4 and tp == 4 and seqs == tp
    length = group * rows
    part_rows = qkv_weight.shape[1]
    cols = qkv_weight.shape[2]
    heads = cols // DH
    units = geglu_weight.shape[2]
    assert units == width and 4 * cols == width and H == heads * tp

    with jax.named_scope("pack_weights"):
        first = jnp.concatenate(
            [qkv_weight[0], qkv_weight[1], qkv_weight[2], out_weight.T], axis=1
        )
        parts = jnp.concatenate(
            [first[None], geglu_weight, down_weight.T[None]], axis=0
        )
        own_bias = jnp.concatenate([qv_bias.reshape(1, -1), geglu_bias.reshape(1, -1)], axis=1)
        own_norm = jnp.concatenate([norm_gains, norm_biases, out_biases], axis=0)

    with jax.named_scope("gather_weights"):
        by_block = lax.all_gather(parts, "tp", axis=0)
        swapped = lax.all_to_all(by_block, "ctx", split_axis=0, concat_axis=0)
        w = lax.all_gather(swapped, "shard", axis=0)
        w = w.transpose(2, 0, 1, 3, 4).reshape(4, shards * group * part_rows, width)
        biases = lax.all_gather(own_bias, "tp", axis=0, tiled=True)
        biases = lax.dynamic_slice_in_dim(biases, c, 1, 0).astype(F32)
        norms = lax.all_gather(own_norm, ("shard", "ctx"), axis=1, tiled=True).astype(F32)
    qv = biases[:, : 2 * cols].reshape(2, cols)
    vec = jnp.concatenate([norms, biases[:, 2 * cols :].reshape(2, units)], axis=0)

    x_own = lax.dynamic_index_in_dim(tokens_in, z, 0, keepdims=False)
    cot_own = lax.dynamic_index_in_dim(cotangent, z, 0, keepdims=False)
    lengths = lax.dynamic_slice_in_dim(doc_lengths, z, 1, 0)
    xs = lax.all_gather(x_own, "ctx", axis=0, tiled=True)
    slopes = jnp.asarray([alibi_slopes(H)], F32)

    head_shape = sds((heads, length, DH), BF16)
    mixed, probs, q, k, v = pl.pallas_call(
        functools.partial(attention_forward, heads),
        out_shape=[sds((length, cols), BF16), sds((heads, length, length), BF16)] + [head_shape] * 3,
        in_specs=[smem(), smem()] + vmem(3),
        out_specs=vmem(5),
        scratch_shapes=[pltpu.VMEM((256, length), F32)],
        compiler_params=pltpu.CompilerParams(vmem_limit_bytes=48 * MB),
        name="attention_forward",
    )(lengths, slopes, xs, w[0], qv)

    block = (rows, width)
    stack = (group, rows, width)
    dma = lambda *shape: pltpu.SemaphoreType.DMA(shape)
    lout, dres1, grads, gout, dmixed, small = pl.pallas_call(
        middle,
        out_shape=[
            sds(block, BF16), sds(block, F32), sds((3, width, width), BF16),
            sds((width, cols), BF16), sds((group, rows, cols), BF16), sds((8, width), F32),
        ],
        in_specs=vmem(5),
        out_specs=vmem(6),
        scratch_shapes=[
            pltpu.VMEM((width, cols), BF16), pltpu.VMEM((3,) + stack, BF16),
        ] + [pltpu.VMEM(stack, BF16)] * 5 + [pltpu.VMEM((3,) + block, BF16)] * 6 + [
            pltpu.VMEM(block, F32)
        ] * 6 + [
            pltpu.VMEM((rows, 1), F32), pltpu.VMEM(block, F32),
            pltpu.VMEM((6, 8, width), F32), pltpu.VMEM((2, 8, width), F32),
            pltpu.VMEM((4, 8, width), F32),
        ] + [dma(3, NCH)] * 12 + [dma(2)] * 2,
        compiler_params=pltpu.CompilerParams(
            collective_id=0, has_side_effects=True, vmem_limit_bytes=58 * MB
        ),
        name="middle",
    )(x_own, cot_own, mixed.reshape(group, rows, cols), w, vec)

    grad_w, d_in, bias_grad = pl.pallas_call(
        functools.partial(attention_backward, heads),
        out_shape=[
            sds((width, 3 * cols), BF16), sds((length, width), BF16), sds((1, 3 * cols), F32)
        ],
        in_specs=vmem(8),
        out_specs=vmem(3),
        scratch_shapes=[
            pltpu.VMEM((length, 3 * cols), BF16),
            pltpu.VMEM((heads, DH, length), F32), pltpu.VMEM((heads, DH, length), F32),
        ],
        compiler_params=pltpu.CompilerParams(vmem_limit_bytes=48 * MB),
        name="attention_backward",
    )(dmixed.reshape(length, cols), mixed, probs, q, k, v, xs, w[0])

    with jax.named_scope("outputs"):
        input_sum = lax.psum_scatter(d_in, "ctx", scatter_dimension=0, tiled=True)
        input_own = (input_sum.astype(F32) + dres1).astype(BF16)
        input_grad = lax.all_gather(input_own, "tp", axis=0).astype(F32)
        layer_out = lax.all_gather(lout, "tp", axis=0)

    with jax.named_scope("scatter_grads"):
        first_grad = jnp.concatenate([grad_w, gout], axis=1)
        packed = jnp.concatenate([first_grad[None], grads], axis=0)
        packed = packed.reshape(4, shards, group, part_rows, width).transpose(1, 2, 0, 3, 4)
        mine = lax.psum_scatter(packed, "shard", scatter_dimension=0, tiled=False)
        mine = lax.all_to_all(mine, "ctx", split_axis=0, concat_axis=0)
        mine = lax.psum_scatter(mine, "tp", scatter_dimension=0, tiled=False)
        mine = mine.astype(F32)
        grad_qkv = jnp.stack([mine[0, :, i * cols : (i + 1) * cols] for i in range(3)])
        grad_out = mine[0, :, 3 * cols :].T
        grad_geglu = mine[1:3]
        grad_down = mine[3].T
        col = jnp.concatenate(
            [bias_grad[:, :cols], bias_grad[:, 2 * cols :], small[6:7], small[7:8]], axis=1
        )
        col = lax.psum_scatter(
            jnp.zeros((group, col.shape[1]), F32) + jnp.where(
                jnp.arange(group)[:, None] == c, col, 0.0),
            "tp", scatter_dimension=0, tiled=True)
        col = lax.psum(col, ("shard", "ctx"))
        norm_grad = lax.psum(small[:6], ("shard", "tp"))
        me = lax.axis_index("shard") * group + c
        norm_grad = lax.dynamic_slice_in_dim(norm_grad, me * part_rows, part_rows, 1)
    return (
        layer_out,
        input_grad,
        grad_qkv,
        col[:, : 2 * cols].reshape(2, cols),
        grad_out,
        grad_geglu,
        col[:, 2 * cols :].reshape(2, units),
        grad_down,
        norm_grad[0:2],
        norm_grad[2:4],
        norm_grad[4:6],
    )


def solution(mesh):
    in_specs = (
        P("shard", "ctx", None),
        P(None, ("shard", "ctx"), "tp"),
        P(None, "tp"),
        P("tp", ("shard", "ctx")),
        P(None, ("shard", "ctx"), "tp"),
        P(None, "tp"),
        P("tp", ("shard", "ctx")),
        P(None, ("shard", "ctx")),
        P(None, ("shard", "ctx")),
        P(None, ("shard", "ctx")),
        P("shard", None),
        P("shard", "ctx", None),
    )
    out_specs = (
        P("shard", "ctx", None),
        P("shard", "ctx", None),
        P(None, ("shard", "ctx"), "tp"),
        P(None, "tp"),
        P("tp", ("shard", "ctx")),
        P(None, ("shard", "ctx"), "tp"),
        P(None, "tp"),
        P("tp", ("shard", "ctx")),
        P(None, ("shard", "ctx")),
        P(None, ("shard", "ctx")),
        P(None, ("shard", "ctx")),
    )
    return jax.shard_map(
        on_device, mesh=mesh, in_specs=in_specs, out_specs=out_specs, check_vma=False
    )
```

time: 1210 us -> 518 us (0.43)
  local copies, waits for them, and re-layouts: 394 us -> 22.9 us
  waiting for transfers between devices: 571 us -> 207 us
  Pallas kernels: 0 us -> 103 us
  matrix products: 85.5 us -> 0 us
  blocking collectives: 83.8 us -> 154 us
  other arithmetic: 48.1 us -> 16 us
    psum x4 -> x0, waiting for transfers between devices: 372 us -> none  [the longest x1 120 us: on_device(): lax.psum(plain_dot(hidden, w_down), 'tp') + bias_rows[1].astype(jnp.float32)]
    unnamed x170 -> x40, local copies, waits for them, and re-layouts: 382 us -> 11.1 us
    pallas_call x0 -> x3, Pallas kernels: none -> 103 us  [the longest x1 74.4 us: on_device(): pl.pallas_call(middle, out_shape=[sds(block, BF16), sds(block, F32), sds(...]
    all_gather x4 -> x5, waiting for transfers between devices: 11.3 us -> 104 us  [the longest x1 53.3 us: on_device(): by_block = lax.all_gather(parts, 'tp', axis=0)]
    unnamed x24 -> x8, waiting for transfers between devices: 84.9 us -> 0.64 us
    dot_general x26 -> x0, matrix products: 83.9 us -> none  [the longest x7 23.7 us: plain_dot(): return jnp.dot(left, right, preferred_element_type=jnp.float32)]
    all_to_all x0 -> x2, blocking collectives: none -> 66 us  [the longest x1 33 us: on_device(): mine = lax.all_to_all(mine, 'ctx', split_axis=0, concat_axis=0)]
    psum x1 -> x2, blocking collectives: 9.33 us -> 46.9 us  [the longest x1 34.1 us: on_device(): norm_grad = lax.psum(small[:6], ('shard', 'tp'))]
  transfers between devices with their start and end apart: 17 -> 8, of which waited for: 11 -> 6; matrix products, arithmetic and copies ran while one was open for 27% -> 4% of each run, Pallas kernels for 0% -> 0%
where the time goes in v1:
time: 518 us
  waiting for transfers between devices  207 us (40%)
  blocking collectives  154 us (30%)
  Pallas kernels  103 us (20%)
  local copies, waits for them, and re-layouts  22.9 us (4%)
  other arithmetic  16 us (3%)
  between operations  14.4 us (3%)
    pallas_call x1, Pallas kernels, on_device(): pl.pallas_call(middle, out_shape=[sds(block, BF16), sds(block, F32), sds(...  74.4 us
    reduce_scatter x1, waiting for transfers between devices, on_device(): mine = lax.psum_scatter(packed, 'shard', scatter_dimension=0, tiled=False)  60.4 us
    all_gather x1, waiting for transfers between devices, on_device(): by_block = lax.all_gather(parts, 'tp', axis=0)  53.3 us
    psum x1, blocking collectives, on_device(): norm_grad = lax.psum(small[:6], ('shard', 'tp'))  34.1 us
    all_gather x1, waiting for transfers between devices, on_device(): w = lax.all_gather(swapped, 'shard', axis=0)  33.6 us
    all_to_all x1, blocking collectives, on_device(): mine = lax.all_to_all(mine, 'ctx', split_axis=0, concat_axis=0)  33 us
    all_to_all x1, blocking collectives, on_device(): swapped = lax.all_to_all(by_block, 'ctx', split_axis=0, concat_axis=0)  33 us
    reduce_scatter x1, waiting for transfers between devices, on_device(): input_sum = lax.psum_scatter(d_in, 'ctx', scatter_dimension=0, tiled=True)  22.1 us
  transfers between devices with their start and end apart: 8, of which 6 were waited for; matrix products, arithmetic and copies ran while one was open for 4% of the time, Pallas kernels for 0%

profile of v1, /device:TPU:0, one launch (start us, length us, event | category | flops | bytes accessed | tf_op | source)
XLA Modules:
  0.0 517.6 jit_solution(14554230336455007343)
XLA Ops:
  7.2 1.0 slice_bitcast_fusion.5
  8.2 0.9 copy.36
  9.1 0.1 maximum_bitcast_fusion.1
  9.2 1.9 pad_maximum_fusion.1
  11.2 53.3 %all-gather.15.cloned.1.call-done = bf16[16,96,768]{2,1,0:T(8,128)(2,1)} async-done(((bf16[4,96,768]{2,1,0:T(8,128)(2,1)}), bf16[16,96,768]{2,1,0:T(8,128)(2,1)}) %all-gather.15.cloned.1.call-update) | async-done | bytes 2359312 | tf_op jit(solution)/shard_map/gather_weights/all_gather | solution.py:436
  64.5 33.0 %all_to_all.10 = bf16[4,4,96,768]{3,2,1,0:T(8,128)(2,1)} all-to-all(bf16[4,4,96,768]{3,2,1,0:T(8,128)(2,1)} %bitcast.77), channel_id=1, replica_groups=mesh['shard'=2,'ctx'=4,'tp'=4] {'ctx'}, dimensions={0} | all-to-all | bytes 4718592 | tf_op jit(solution)/shard_map/gather_weights/all_to_all | solution.py:437
  97.6 0.8 constant_dynamic-slice_fusion.2
  98.6 13.1 %all-gather.5 = bf16[4,1,1920]{2,1,0:T(2,128)(2,1)S(1)} all-gather(bf16[1,1,1920]{2,1,0:T(2,128)(2,1)S(1)} %maximum_bitcast_fusion.2), channel_id=1, replica_groups=mesh['shard'=2,'ctx'=4,'tp'=4] {'tp'}, dimensions={0}, use_global_device_ids=true | all-gather | bytes 19200 | tf_op jit(solution)/shard_map/gather_weights/all_gather | solution.py:440
  111.9 8.9 %all-gather.6 = bf16[8,96,6]{1,2,0:T(8,128)(2,1)S(1)} all-gather(bf16[1,96,6]{1,2,0:T(8,128)(2,1)S(1)} %maximum_bitcast_fusion.3), channel_id=1, replica_groups=mesh['shard'=2,'ctx'=4,'tp'=4] {'shard','ctx'}, dimensions={0}, use_global_device_ids=true | all-gather | bytes 10368 | tf_op jit(solution)/shard_map/gather_weights/all_gather | solution.py:442
  120.9 0.7 constant_dynamic-slice_fusion.1.lengths
  121.6 0.6 pad_maximum_fusion.3.vec
  122.2 0.8 fusion.5.x
  123.0 1.8 dynamic-slice_bitcast_fusion.cot
  124.7 33.6 %all-gather.17.cloned.1.call-done = bf16[8,4,96,768]{3,2,1,0:T(8,128)(2,1)} async-done(((bf16[4,4,96,768]{3,2,1,0:T(8,128)(2,1)}), bf16[8,4,96,768]{3,2,1,0:T(8,128)(2,1)}) %all-gather.17.cloned.1.call-update) | async-done | bytes 4718608 | tf_op jit(solution)/shard_map/gather_weights/all_gather | solution.py:438
  158.3 2.7 copy.48
  161.0 2.2 copy-done.7
  163.3 16.8 %all-gather.13.cloned.1.call-done = bf16[1,1024,768]{2,1,0:T(8,128)(2,1)} async-done(((bf16[1,256,768]{2,1,0:T(8,128)(2,1)}), bf16[1,1024,768]{2,1,0:T(8,128)(2,1)}) %all-gather.13.cloned.1.call-update) | async-done | bytes 1572880 | tf_op jit(solution)/shard_map/all_gather | solution.py:449
  180.1 1.4 copy-done.1
  181.6 14.3 %attention_forward.1 = (bf16[1024,192]{1,0:T(8,128)(2,1)S(1)}, bf16[3,1024,1024]{2,1,0:T(8,128)(2,1)}, bf16[3,1024,64]{2,1,0:T(8,128)(2,1)S(1)}, bf16[3,1024,64]...) custom-call(s32[1,8]{1,0:T(1,128)S(1)} %constant_dynamic-slice_fusion.1.lengths, f32[1,12]{1,0:T(1,128)S(1)} %copy-done.6, ...), custom_call_target="tpu_custom_call" | custom-call | tf_op jit(solution)/shard_map/attention_forward/pallas_call | solution.py:453
  195.8 0.8 copy-done.2
  196.6 74.4 %middle.1 = (bf16[256,768]{1,0:T(8,128)(2,1)}, f32[256,768]{1,0:T(8,128)}, bf16[3,768,768]{2,1,0:T(8,128)(2,1)}, bf16[768,192]{1,0:T(8,128)(2,1)}, bf16[4,256,192]{2,1,0:T(8,128)(2,1)}, /*index=5*/f32[8,768]{1,0:T(8,128)}) custom-call(bf16[256,768]{1,0:T(8,128)(2,1)} %fusion.5.x, bf16[256,768]{1,0:T(8,128)(2,1)} %dynamic-slice_bitcast_fusion.cot, ...), custom_call_target="tpu_custom_call" | custom-call | tf_op jit(solution)/shard_map/middle/pallas_call | solution.py:466
  271.0 1.0 copy-done.5
  272.1 14.3 %attention_backward.1 = (bf16[768,576]{1,0:T(8,128)(2,1)S(1)}, bf16[1024,768]{1,0:T(8,128)(2,1)}, f32[1,576]{1,0:T(1,128)S(1)}) custom-call(bf16[1024,192]{1,0:T(8,128)(2,1)S(1)} %bitcast.70, bf16[1024,192]{1,0:T(8,128)(2,1)S(1)} %copy-done.3, bf16[3,1024,1024]{2,1,0:T(8,128)(2,1)} %get-tuple-element.28.probs, bf16[3,1024,64]{2,1,0:T(8,128)(2,1)S(1)} %get-tuple-element.29.q, ...), custom_call_target="tpu_custom_call" | custom-call | tf_op jit(solution)/shard_map/attention_backward/pallas_call | solution.py:489
  286.4 0.9 copy-done.4
  287.4 1.5 pad_maximum_fusion
  288.9 4.5 maximum_bitcast_fusion
  293.5 0.5 all-gather.19.cloned.1.call-update
  294.1 22.1 %reduce-scatter.4.cloned.1.call-done = bf16[256,768]{1,0:T(8,128)(2,1)} async-done(((bf16[1024,768]{1,0:T(8,128)(2,1)}), bf16[256,768]{1,0:T(8,128)(2,1)}) %reduce-scatter.4.cloned.1.call-update) | async-done | bytes 393232 | tf_op jit(solution)/shard_map/outputs/reduce_scatter | solution.py:505
  316.2 1.8 add_convert_fusion
  318.1 60.4 %reduce-scatter.6.cloned.1.call-done = bf16[1,4,4,96,768]{4,3,2,1,0:T(8,128)(2,1)} async-done(((bf16[2,4,4,96,768]{4,3,2,1,0:T(8,128)(2,1)}), bf16[1,4,4,96,768]{4,3,2,1,0:T(8,128)(2,1)}) %reduce-scatter.6.cloned.1.call-update) | async-done | bytes 2359312 | tf_op jit(solution)/shard_map/scatter_grads/reduce_scatter | solution.py:514
  378.4 33.0 %all_to_all.11 = bf16[4,4,96,768]{3,2,1,0:T(8,128)(2,1)} all-to-all(bf16[4,4,96,768]{3,2,1,0:T(8,128)(2,1)} %bitcast.76), channel_id=1, replica_groups=mesh['shard'=2,'ctx'=4,'tp'=4] {'ctx'}, dimensions={0} | all-to-all | bytes 4718592 | tf_op jit(solution)/shard_map/scatter_grads/all_to_all | solution.py:515
  411.5 0.6 copy-done.16
  412.1 0.6 dynamic-slice.1
  412.9 19.2 %all-reduce = f32[4,1920]{1,0:T(4,128)S(1)} all-reduce(f32[4,1920]{1,0:T(4,128)S(1)} %broadcast_select_fusion), channel_id=10, replica_groups=mesh['shard'=2,'ctx'=4,'tp'=4] {'tp'}, use_global_device_ids=true, to_apply=%region_3.4.clone | all-reduce | flops 7680 | bytes 61440
  432.1 0.7 constant_dynamic-slice_fusion.3
  432.8 12.8 %psum.14 = f32[1,1920]{1,0:T(1,128)S(1)} all-reduce(f32[1,1920]{1,0:T(1,128)S(1)} %constant_dynamic-slice_fusion.3), channel_id=1, replica_groups=mesh['shard'=2,'ctx'=4,'tp'=4] {'shard','ctx'}, use_global_device_ids=true, to_apply=%region_4.5 | all-reduce | flops 1920 | bytes 15360 | tf_op jit(solution)/shard_map/scatter_grads/psum | solution.py:529
  445.6 0.6 reshape.72
  446.2 0.7 reshape.71
  446.9 34.1 %psum.15 = f32[6,768]{1,0:T(8,128)S(1)} all-reduce(f32[6,768]{1,0:T(8,128)S(1)} %bitcast.83), channel_id=1, replica_groups=mesh['shard'=2,'ctx'=4,'tp'=4] {'shard','tp'}, use_global_device_ids=true, to_apply=%region_5.6 | all-reduce | flops 4608 | bytes 36864 | tf_op jit(solution)/shard_map/scatter_grads/psum | solution.py:530
  481.0 0.6 fusion.3
  481.6 3.3 convert.1
  485.0 20.2 %reduce-scatter.8.cloned.1.call-done = bf16[1,4,96,768]{3,2,1,0:T(8,128)(2,1)} async-done(((bf16[4,4,96,768]{3,2,1,0:T(8,128)(2,1)}), bf16[1,4,96,768]{3,2,1,0:T(8,128)(2,1)}) %reduce-scatter.8.cloned.1.call-update) | async-done | bytes 589840 | tf_op jit(solution)/shard_map/scatter_grads/reduce_scatter | solution.py:516
  505.1 1.2 fusion.1
  506.4 0.9 slice_bitcast_fusion
  507.3 0.7 slice_bitcast_fusion.1
  508.1 0.7 copy.41
  508.8 0.7 pad_maximum_fusion.2
  509.6 1.1 copy.50
  (67 shorter events, 1.4 us)
Async XLA Ops:
  7.2 90.4 %copy-start = (bf16[4,256,768]{2,1,0:T(8,128)(2,1)S(1)}, bf16[4,256,768]{2,1,0:T(8,128)(2,1)}, u32[]{:S(2)}) copy-start(bf16[4,256,768]{2,1,0:T(8,128)(2,1)} %param.13) | copy-start | bytes 4718596
  7.2 57.3 %all-gather.15.cloned.1.call-start = ((), (), s32[]{:S(2)}) async-start(), calls=%async_computation.9 | async-start | bytes 2949120 | tf_op jit(solution)/shard_map/gather_weights/all_gather | solution.py:436
  11.2 147.1 %all-gather.17.cloned.1.call-start = ((), (), s32[]{:S(2)}) async-start(), calls=%async_computation.10 | async-start | bytes 7077888 | tf_op jit(solution)/shard_map/gather_weights/all_gather | solution.py:438
  97.5 1.0 copy-start.11
  97.5 1.0 copy-start.12
  97.5 14.4 %copy-start.13 = (bf16[2,96]{1,0:T(2,128)(2,1)S(1)}, bf16[2,96]{1,0:T(2,128)(2,1)}, u32[]{:S(2)}) copy-start(bf16[2,96]{1,0:T(2,128)(2,1)} %param.22) | copy-start | bytes 1156
  97.5 14.4 %copy-start.14 = (bf16[2,96]{1,0:T(2,128)(2,1)S(1)}, bf16[2,96]{1,0:T(2,128)(2,1)}, u32[]{:S(2)}) copy-start(bf16[2,96]{1,0:T(2,128)(2,1)} %param.21) | copy-start | bytes 1156
  97.5 14.4 %copy-start.15 = (bf16[2,96]{1,0:T(2,128)(2,1)S(1)}, bf16[2,96]{1,0:T(2,128)(2,1)}, u32[]{:S(2)}) copy-start(bf16[2,96]{1,0:T(2,128)(2,1)} %param.20) | copy-start | bytes 1156
  97.5 82.6 %all-gather.13.cloned.1.call-start = ((), (), s32[]{:S(2)}) async-start(), calls=%async_computation.8 | async-start | bytes 1966080 | tf_op jit(solution)/shard_map/all_gather | solution.py:449
  98.4 217.8 %reduce-scatter.4.cloned.1.call-start = ((), (), s32[]{:S(2)}) async-start(), calls=%async_computation.5 | async-start | bytes 1966080 | tf_op jit(solution)/shard_map/outputs/reduce_scatter | solution.py:505
  161.0 2.2 copy-start.7
  161.0 19.1 %copy-start.6 = (f32[1,12]{1,0:T(1,128)S(1)}, f32[1,12]{1,0:T(1,128)}, u32[]{:S(2)}) copy-start(f32[1,12]{1,0:T(1,128)} %constant.31.clone.slopes) | copy-start | bytes 148
  180.1 1.4 copy-start.1
  195.8 0.8 copy-start.2
  196.6 74.4 %copy-start.3 = (bf16[1024,192]{1,0:T(8,128)(2,1)S(1)}, bf16[1024,192]{1,0:T(8,128)(2,1)}, u32[]{:S(2)}) copy-start(bf16[1024,192]{1,0:T(8,128)(2,1)} %copy-done.2) | copy-start | bytes 1179652
  271.0 1.0 copy-start.5
  286.3 0.9 copy-start.4
  287.3 91.1 %reduce-scatter.6.cloned.1.call-start = ((), (), s32[]{:S(2)}) async-start(), calls=%async_computation.6 | async-start | bytes 7077888 | tf_op jit(solution)/shard_map/scatter_grads/reduce_scatter | solution.py:514
  293.4 22.8 %copy-start.9 = (f32[256,768]{1,0:T(8,128)S(1)}, f32[256,768]{1,0:T(8,128)}, u32[]{:S(2)}) copy-start(f32[256,768]{1,0:T(8,128)} %get-tuple-element.33) | copy-start | bytes 2359300
  293.4 188.2 %all-gather.19.cloned.1.call-start = ((), (), s32[]{:S(2)}) async-start(), calls=%async_computation.11 | async-start | bytes 1966080 | tf_op jit(solution)/shard_map/outputs/all_gather | solution.py:508
  294.0 187.6 %all-gather.21.cloned.1.call-start = ((), (), s32[]{:S(2)}) async-start(), calls=%async_computation.12 | async-start | bytes 1966080 | tf_op jit(solution)/shard_map/outputs/all_gather | solution.py:507
  318.0 187.1 %reduce-scatter.8.cloned.1.call-start = ((), (), s32[]{:S(2)}) async-start(), calls=%async_computation.7 | async-start | bytes 2949120 | tf_op jit(solution)/shard_map/scatter_grads/reduce_scatter | solution.py:516
  411.4 0.7 copy-start.16
  411.4 1.2 copy-start.10
  506.4 3.2 copy-start.8
Sparse Core Ops, SparseCore 0:
  11.3 53.1 all-gather.14
  97.6 60.6 all-gather.16
  160.4 19.6 all-gather.12
  287.4 28.6 reduce-scatter.3
  318.4 59.9 reduce-scatter.5
  379.9 37.1 all-gather.18
  419.2 36.4 all-gather.20
  457.9 47.1 reduce-scatter.7

commit v2 on v1

--- a/solution.py
+++ b/solution.py
@@ -44,56 +44,84 @@
     return [pl.BlockSpec(memory_space=pltpu.VMEM)] * count
 
 
+def project_heads(heads, x_rows, rows, w, bias, q_out, k_out, v_out):
+    cols = heads * DH
+    for part, out in enumerate((q_out, k_out, v_out)):
+        y = dot(x_rows, w[:, part * cols : (part + 1) * cols])
+        if part != 1:
+            y = y + bias[part // 2 : part // 2 + 1, :]
+        y = y.astype(BF16)
+        if part == 0:
+            y = y * BF16(1.0 / math.sqrt(DH))
+        for i in range(heads):
+            out[i, rows, :] = y[:, i * DH : (i + 1) * DH]
+
+
+def segments(lengths, pos):
+    seg = jnp.zeros(pos.shape, jnp.int32)
+    end = 0
+    for k in range(lengths.shape[1]):
+        end = end + lengths[0, k]
+        seg = seg + (pos >= end).astype(jnp.int32)
+    return seg
+
+
+def attend_rows(heads, start, step, lengths, slopes, q, k, v, probs, mixed, far):
+    length = k.shape[1]
+    mine = lax.axis_index("ctx") * heads
+    rows = pl.ds(start, step)
+    key_pos = lax.broadcasted_iota(jnp.int32, (1, length), 1)
+    pos = start + lax.broadcasted_iota(jnp.int32, (step, 1), 0)
+    same = segments(lengths, pos) == segments(lengths, key_pos)
+    far[...] = jnp.where(same, jnp.abs(pos - key_pos).astype(F32), 1e33)
+    for i in range(heads):
+        s = dot_nt(q[i, rows, :], k[i]) - slopes[0, mine + i] * far[...]
+        p = jnp.exp(s - jnp.max(s, axis=-1, keepdims=True))
+        p = (p * (1.0 / jnp.sum(p, axis=-1, keepdims=True))).astype(BF16)
+        probs[i, rows, :] = p
+        mixed[rows, i * DH : (i + 1) * DH] = dot(p, v[i]).astype(BF16)
+
+
 def attention_forward(
     heads, lengths, slopes, xs, w, bias, mixed, probs, q_out, k_out, v_out, far
 ):
-    length = xs.shape[0]
     step = 256
-    cols = heads * DH
-    mine = lax.axis_index("ctx") * heads
 
     def project(r, carry):
         rows = pl.ds(pl.multiple_of(r * step, step), step)
-        x_rows = xs[rows, :]
-        for part, out in enumerate((q_out, k_out, v_out)):
-            y = dot(x_rows, w[:, part * cols : (part + 1) * cols])
-            if part != 1:
-                y = y + bias[part // 2 : part // 2 + 1, :]
-            y = y.astype(BF16)
-            if part == 0:
-                y = y * BF16(1.0 / math.sqrt(DH))
-            for i in range(heads):
-                out[i, rows, :] = y[:, i * DH : (i + 1) * DH]
+        project_heads(heads, xs[rows, :], rows, w, bias, q_out, k_out, v_out)
         return carry
-
-    lax.fori_loop(0, length // step, project, 0)
-
-    def segments(pos):
-        seg = jnp.zeros(pos.shape, jnp.int32)
-        end = 0
-        for k in range(lengths.shape[1]):
-            end = end + lengths[0, k]
-            seg = seg + (pos >= end).astype(jnp.int32)
-        return seg
-
-    key_pos = lax.broadcasted_iota(jnp.int32, (1, length), 1)
-    key_seg = segments(key_pos)
 
     def attend(r, carry):
         start = pl.multiple_of(r * step, step)
-        rows = pl.ds(start, step)
-        pos = start + lax.broadcasted_iota(jnp.int32, (step, 1), 0)
-        same = segments(pos) == key_seg
-        far[...] = jnp.where(same, jnp.abs(pos - key_pos).astype(F32), 1e33)
-        for i in range(heads):
-            s = dot_nt(q_out[i, rows, :], k_out[i]) - slopes[0, mine + i] * far[...]
-            p = jnp.exp(s - jnp.max(s, axis=-1, keepdims=True))
-            p = (p * (1.0 / jnp.sum(p, axis=-1, keepdims=True))).astype(BF16)
-            probs[i, rows, :] = p
-            mixed[rows, i * DH : (i + 1) * DH] = dot(p, v_out[i]).astype(BF16)
+        attend_rows(
+            heads, start, step, lengths, slopes, q_out, k_out, v_out, probs, mixed, far)
         return carry
 
-    lax.fori_loop(0, length // step, attend, 0)
+    lax.fori_loop(0, xs.shape[0] // step, project, 0)
+    lax.fori_loop(0, xs.shape[0] // step, attend, 0)
+
+
+def attend_back(heads, rows, dmixed, mixed, probs, q, k, v, dqkv, dk_acc, dv_acc):
+    for i in range(heads):
+        own = slice(i * DH, (i + 1) * DH)
+        d_out = dmixed[rows, own]
+        row_dot = jnp.sum(
+            d_out.astype(F32) * mixed[rows, own].astype(F32), axis=-1, keepdims=True
+        )
+        p = probs[i, rows, :]
+        dp = dot_nt(d_out, v[i])
+        ds = (p.astype(F32) * (dp - row_dot)).astype(BF16)
+        dqkv[rows, own] = (dot(ds, k[i]) * (1.0 / math.sqrt(DH))).astype(BF16)
+        dk_acc[i] += dot_tn(q[i, rows, :], ds)
+        dv_acc[i] += dot_tn(d_out, p)
+
+
+def spread_heads(heads, dqkv, dk_acc, dv_acc):
+    cols = heads * DH
+    for i in range(heads):
+        dqkv[:, cols + i * DH : cols + (i + 1) * DH] = dk_acc[i].T.astype(BF16)
+        dqkv[:, 2 * cols + i * DH : 2 * cols + (i + 1) * DH] = dv_acc[i].T.astype(BF16)
 
 
 def attention_backward(
@@ -107,24 +135,11 @@
 
     def rows_back(r, carry):
         rows = pl.ds(pl.multiple_of(r * step, step), step)
-        for i in range(heads):
-            own = slice(i * DH, (i + 1) * DH)
-            d_out = dmixed[rows, own]
-            row_dot = jnp.sum(
-                d_out.astype(F32) * mixed[rows, own].astype(F32), axis=-1, keepdims=True
-            )
-            p = probs[i, rows, :]
-            dp = dot_nt(d_out, v[i])
-            ds = (p.astype(F32) * (dp - row_dot)).astype(BF16)
-            dqkv[rows, own] = (dot(ds, k[i]) * (1.0 / math.sqrt(DH))).astype(BF16)
-            dk_acc[i] += dot_tn(q[i, rows, :], ds)
-            dv_acc[i] += dot_tn(d_out, p)
+        attend_back(heads, rows, dmixed, mixed, probs, q, k, v, dqkv, dk_acc, dv_acc)
         return carry
 
     lax.fori_loop(0, length // step, rows_back, 0)
-    for i in range(heads):
-        dqkv[:, cols + i * DH : cols + (i + 1) * DH] = dk_acc[i].T.astype(BF16)
-        dqkv[:, 2 * cols + i * DH : 2 * cols + (i + 1) * DH] = dv_acc[i].T.astype(BF16)
+    spread_heads(heads, dqkv, dk_acc, dv_acc)
 
     def finish(r, total):
         rows = pl.ds(pl.multiple_of(r * step, step), step)
@@ -140,28 +155,349 @@
         grad_w[:, own] = dot_tn(xs[...], dqkv[:, own]).astype(BF16)
 
 
+class Links:
+    def __init__(self):
+        self.started = []
+
+    def copy(self, src, dst, send, recv, peer):
+        return pltpu.make_async_remote_copy(
+            src_ref=src, dst_ref=dst, send_sem=send, recv_sem=recv,
+            device_id=peer, device_id_type=MESH,
+        )
+
+    def start(self, src, dst, send, recv, peer):
+        copy = self.copy(src, dst, send, recv, peer)
+        copy.start()
+        self.started.append(copy)
+        return copy
+
+    def drain(self):
+        for copy in self.started:
+            copy.wait_send()
+        self.started = []
+
+
+def greet(peers):
+    barrier = pltpu.get_barrier_semaphore()
+    for peer in peers:
+        pl.semaphore_signal(barrier, inc=1, device_id=peer, device_id_type=MESH)
+    pl.semaphore_wait(barrier, len(peers))
+
+
+def places():
+    c = lax.axis_index("ctx")
+    flip = 1 - 2 * (c % 2)
+    ynb = (c + 2) % 4
+    return c, c + flip, ynb, ynb + flip
+
+
+class LineGather:
+    def __init__(self, blocks, up, down, recv):
+        self.blocks, self.up, self.down, self.recv = blocks, up, down, recv
+        self.z = lax.axis_index("tp")
+        self.last = blocks.shape[0] - 1
+
+    def _copy(self, j, sem, peer):
+        block = self.blocks.at[j]
+        return pltpu.make_async_remote_copy(
+            src_ref=block, dst_ref=block, send_sem=sem.at[j], recv_sem=self.recv.at[j],
+            device_id={"tp": peer}, device_id_type=MESH,
+        )
+
+    def hop(self, d):
+        z, last = self.z, self.last
+        for side, j in ((0, z - d), (1, z + d)):
+            here = (j >= 0) if side == 0 else (j <= last)
+            edge = (z < last) if side == 0 else (z > 0)
+
+            @pl.when(here)
+            def _(side=side, j=j, edge=edge):
+                sem = self.up if side == 0 else self.down
+                if d:
+                    self._copy(j, sem, z).wait_recv()
+                if d < last:
+                    @pl.when(edge)
+                    def _():
+                        self._copy(j, sem, z + 1 if side == 0 else z - 1).start()
+
+    def drain(self):
+        z, last = self.z, self.last
+        for d in range(last):
+            for side, j in ((0, z - d), (1, z + d)):
+                here = (j >= 0) if side == 0 else (j <= last)
+                edge = (z < last) if side == 0 else (z > 0)
+
+                @pl.when(jnp.logical_and(here, edge))
+                def _(side=side, j=j):
+                    self._copy(j, self.up if side == 0 else self.down, z).wait_send()
+
+
+def front(
+    heads, lengths, slopes, x, p0, pr,
+    xs, w0, w, vec, mixed, probs, q, k, v,
+    zb0, zbr, wb0, qv, far,
+    xg_s, xg_r, zs, zr, ys, yr, xs_s, xs_r,
+):
+    c, sib, ynb, dia = places()
+    me = lax.axis_index("shard")
+    z = lax.axis_index("tp")
+    tp = zb0.shape[0]
+    other = 1 - me
+    piece = pr.shape[1]
+    greet([{"ctx": sib}, {"ctx": ynb}, {"ctx": dia}, {"shard": other}]
+          + [{"tp": (z + d) % tp} for d in range(1, tp)])
+    links = Links()
+    src = [p0] + [pr.at[i] for i in range(3)]
+    zb = [zb0] + [zbr.at[i] for i in range(3)]
+    wr = [wb0] + [w.at[i] for i in range(3)]
+
+    def spread(p):
+        for d in range(1, tp):
+            links.start(src[p], zb[p].at[z], zs.at[p, d - 1], zr.at[p, z], {"tp": (z + d) % tp})
+        zb[p].at[z][...] = src[p][...]
+
+    def to_owner(p):
+        for rel, j in enumerate((c, sib, ynb, dia)):
+            @pl.when(j != z)
+            def _(j=j):
+                links.copy(src[p], zb[p].at[j], zs.at[p, 0], zr.at[p, j], {"tp": z}).wait_recv()
+            if rel == 0:
+                wr[p].at[me, c][...] = zb[p].at[c][...]
+            else:
+                links.start(zb[p].at[j], wr[p].at[me, c], ys.at[p, rel - 1], yr.at[p, c], {"ctx": j})
+
+    def to_shard(p):
+        for i, j in enumerate((c, sib, ynb, dia)):
+            slot = wr[p].at[me, j]
+            if i:
+                links.copy(zb[p].at[c], slot, ys.at[p, 0], yr.at[p, j], {"ctx": c}).wait_recv()
+            links.start(slot, slot, xs_s.at[p, i], xs_r.at[p, j], {"shard": other})
+
+    def complete(p):
+        for j in range(4):
+            slot = wr[p].at[other, j]
+            links.copy(slot, slot, xs_s.at[p, 0], xs_r.at[p, j], {"shard": other}).wait_recv()
+
+    xs.at[c][...] = x[...]
+    first = links.start(xs.at[c], xs.at[c], xg_s.at[0], xg_r.at[0], {"ctx": ynb})
+    near = links.start(xs.at[c], xs.at[c], xg_s.at[1], xg_r.at[1], {"ctx": sib})
+    spread(0)
+    to_owner(0)
+    spread(1)
+    first.wait_recv()
+    passed = links.start(xs.at[ynb], xs.at[ynb], xg_s.at[2], xg_r.at[2], {"ctx": sib})
+    to_shard(0)
+    near.wait_recv()
+    passed.wait_recv()
+    complete(0)
+    total = jnp.zeros((p0.shape[0] - piece, p0.shape[1]), F32)
+    for s in range(2):
+        for j in range(4):
+            w0[pl.ds((s * 4 + j) * piece, piece), :] = wb0[s, j, 0:piece, :]
+            total = total + wb0[s, j, piece:, :].astype(F32)
+    one = wb0[0, 0, piece:, :].astype(F32)
+    cols = heads * DH
+    qv[0:1, :] = one[0:1, 0:cols]
+    qv[1:2, :] = one[0:1, cols : 2 * cols]
+    vec[0:6, :] = total[3:9, :]
+    vec[6:8, :] = one[1:3, :]
+    step = x.shape[0]
+
+    def project(r, carry):
+        rows = pl.ds(pl.multiple_of(r * step, step), step)
+        project_heads(heads, xs[r], rows, w0, qv, q, k, v)
+        return carry
+
+    lax.fori_loop(0, 4, project, 0)
+    to_owner(1)
+    spread(2)
+
+    def attend(r, carry):
+        attend_rows(heads, pl.multiple_of(r * step, step), step, lengths, slopes,
+                    q, k, v, probs, mixed, far)
+        return carry
+
+    lax.fori_loop(0, 2, attend, 0)
+    to_shard(1)
+    lax.fori_loop(2, 4, attend, 0)
+    to_owner(2)
+    spread(3)
+    to_shard(2)
+    to_owner(3)
+    to_shard(3)
+    for p in range(1, 4):
+        complete(p)
+    links.drain()
+
+
+def back(
+    heads, dmixed, mixed, probs, q, k, v, xs, w0, grads, gout, small, dres1,
+    out0, outr, input_grad,
+    dqkv, dk_acc, dv_acc, extra, gq, g0, xb0, xbr, sb0, sbr, yb0, ybr, zb0, zbr,
+    snd_r, snd_o, snd_y, rcv_r, rcv_o, rcv_y, own, yacc,
+    gx_s, gx_r, gy_s, gy_r, gz_s, gz_r,
+    rss_r, rsr_r, rss_o, rsr_o, rss_y, rsr_y, lu, ld, lr,
+):
+    c, sib, ynb, dia = places()
+    me = lax.axis_index("shard")
+    z = lax.axis_index("tp")
+    tp = zb0.shape[0]
+    other = 1 - me
+    piece = outr.shape[1]
+    cols = heads * DH
+    rows_own, width = dres1.shape
+    cr = rows_own // NCH
+    greet([{"ctx": sib}, {"ctx": ynb}, {"ctx": dia}, {"shard": other}]
+          + [{"tp": (z + d) % tp} for d in range(1, tp)])
+    links = Links()
+    line = LineGather(input_grad, lu, ld, lr)
+    part = [g0] + [grads.at[i] for i in range(3)]
+    xb = [xb0] + [xbr.at[i] for i in range(3)]
+    sb = [sb0] + [sbr.at[i] for i in range(3)]
+    yb = [yb0] + [ybr.at[i] for i in range(3)]
+    zb = [zb0] + [zbr.at[i] for i in range(3)]
+    out = [out0] + [outr.at[i] for i in range(3)]
+
+    def to_shard(p):
+        for i, j in enumerate((dia, ynb, sib, c)):
+            links.start(part[p].at[other, j], xb[p].at[j], gx_s.at[p, i], gx_r.at[p, j], {"shard": other})
+
+    def to_owner(p):
+        for i, j in enumerate((dia, ynb, sib, c)):
+            links.copy(part[p].at[other, j], xb[p].at[j], gx_s.at[p, 0], gx_r.at[p, j], {"shard": other}).wait_recv()
+            total = part[p].at[me, j][...].astype(F32) + xb[p].at[j][...].astype(F32)
+            if i == 3:
+                yb[p].at[c][...] = total.astype(BF16)
+            else:
+                sb[p].at[j][...] = total.astype(BF16)
+                links.start(sb[p].at[j], yb[p].at[c], gy_s.at[p, i], gy_r.at[p, c], {"ctx": j})
+
+    def away(p, rel, j):
+        return links.copy(yb[p].at[j], zb[p].at[z], gz_s.at[p, rel], gz_r.at[p, z], {"tp": j})
+
+    def to_plane(p):
+        for rel, j in enumerate((c, sib, ynb, dia)):
+            if rel:
+                links.copy(sb[p].at[j], yb[p].at[j], gy_s.at[p, 0], gy_r.at[p, j], {"ctx": j}).wait_recv()
+
+            @pl.when(j != z)
+            def _(rel=rel, j=j):
+                away(p, rel, j).start()
+
+    def total(p):
+        value = yb[p].at[z][...].astype(F32)
+        for d in range(1, tp):
+            t = (z + d) % tp
+            links.copy(yb[p].at[t], zb[p].at[t], gz_s.at[p, 0], gz_r.at[p, t], {"tp": t}).wait_recv()
+            value = value + zb[p].at[t][...].astype(F32)
+        out[p][...] = value
+
+    def chunk(k):
+        return pl.ds(k * cr, cr)
+
+    for p in (1, 2, 3):
+        to_shard(p)
+    dk_acc[...] = jnp.zeros_like(dk_acc)
+    dv_acc[...] = jnp.zeros_like(dv_acc)
+
+    def rows_back(r, carry):
+        rows = pl.ds(pl.multiple_of(r * rows_own, rows_own), rows_own)
+        attend_back(heads, rows, dmixed, mixed, probs, q, k, v, dqkv, dk_acc, dv_acc)
+        return carry
+
+    lax.fori_loop(0, 4, rows_back, 0)
+    spread_heads(heads, dqkv, dk_acc, dv_acc)
+    to_owner(1)
+
+    def piece_in(b, r0, n):
+        rows = pl.ds(pl.multiple_of(b * rows_own + r0, cr), n)
+        return dot_nt(dqkv[rows, :], w0[:, : 3 * cols])
+
+    relays = []
+    outs = []
+    sums = []
+
+    def relay(k):
+        relays[k].wait_recv()
+        snd_y[chunk(k), :] = (yacc[chunk(k), :] + rcv_r[chunk(k), :].astype(F32)).astype(BF16)
+        sums.append(links.start(
+            snd_y.at[chunk(k)], rcv_y.at[chunk(k)], rss_y.at[k], rsr_y.at[k], {"ctx": ynb}))
+
+    for k in range(NCH):
+        snd_r[chunk(k), :] = piece_in(dia, k * cr, cr).astype(BF16)
+        relays.append(links.start(
+            snd_r.at[chunk(k)], rcv_r.at[chunk(k)], rss_r.at[k], rsr_r.at[k], {"ctx": sib}))
+        yacc[chunk(k), :] = piece_in(ynb, k * cr, cr)
+        if k:
+            relay(k - 1)
+    relay(NCH - 1)
+    for k in range(NCH):
+        snd_o[chunk(k), :] = piece_in(sib, k * cr, cr).astype(BF16)
+        outs.append(links.start(
+            snd_o.at[chunk(k)], rcv_o.at[chunk(k)], rss_o.at[k], rsr_o.at[k], {"ctx": sib}))
+    own[...] = piece_in(c, 0, rows_own)
+
+    d_all = dqkv[...]
+    bias = jnp.sum(d_all.astype(F32), axis=0, keepdims=True)
+    for i in range(3):
+        mine = slice(i * cols, (i + 1) * cols)
+        gq[:, mine] = dot_tn(xs[...].reshape(4 * rows_own, width), dqkv[:, mine]).astype(BF16)
+    gq[:, 3 * cols : 4 * cols] = gout[...]
+    extra[...] = jnp.zeros_like(extra)
+    extra[0:1, 0:cols] = bias[:, :cols]
+    extra[0:1, cols : 2 * cols] = bias[:, 2 * cols :]
+    extra[1:3, :] = small[6:8, :]
+    extra[3:9, :] = small[0:6, :]
+    low = extra[...].astype(BF16)
+    for s in range(2):
+        for j in range(4):
+            g0[s, j, 0:piece, :] = gq[pl.ds((s * 4 + j) * piece, piece), :]
+            g0[s, j, piece:, :] = low
+    to_shard(0)
+    to_plane(1)
+    to_owner(2)
+    for k in range(NCH):
+        outs[k].wait_recv()
+        sums[k].wait_recv()
+        value = own[chunk(k), :] + rcv_o[chunk(k), :].astype(F32) + rcv_y[chunk(k), :].astype(F32)
+        input_grad[z, chunk(k), :] = (value + dres1[chunk(k), :]).astype(BF16)
+    line.hop(0)
+    to_plane(2)
+    to_owner(3)
+    line.hop(1)
+    to_plane(3)
+    to_owner(0)
+    line.hop(2)
+    to_plane(0)
+    line.hop(3)
+    for p in (1, 2, 3, 0):
+        total(p)
+    line.drain()
+    for p in range(4):
+        for rel, j in enumerate((c, sib, ynb, dia)):
+            @pl.when(j != z)
+            def _(p=p, rel=rel, j=j):
+                away(p, rel, j).wait_send()
+    links.drain()
+
+
 def middle(
-    x, cot, mixed, w, vec,
+    x, cot, mixed, w0, w, vec,
     lout, dres1, grads, gout, dmixed, small,
     w_out, full, act, pull, hid, dgt, dup,
     snd_r, snd_o, snd_y, rcv_r, rcv_o, rcv_y,
     own, yacc, fa, fb, normed, zh1, r1, dres2, acc, bsum, tiny,
     ags_y, agr_y, ags_c, agr_c, ags_f, agr_f,
-    rss_r, rsr_r, rss_o, rsr_o, rss_y, rsr_y, tiny_s, tiny_r,
+    rss_r, rsr_r, rss_o, rsr_o, rss_y, rsr_y, tiny_s, tiny_r, lu, ld, lr,
 ):
     rows_own = x.shape[0]
     width = x.shape[1]
     cr = rows_own // NCH
-    c = lax.axis_index("ctx")
-    flip = 1 - 2 * (c % 2)
-    sib = c + flip
-    ynb = (c + 2) % 4
-    dia = ynb + flip
-
-    barrier = pltpu.get_barrier_semaphore()
-    for peer in (sib, ynb):
-        pl.semaphore_signal(barrier, inc=1, device_id={"ctx": peer}, device_id_type=MESH)
-    pl.semaphore_wait(barrier, 2)
+    c, sib, ynb, dia = places()
+    z = lax.axis_index("tp")
+    tp = lout.shape[0]
+    greet([{"ctx": sib}, {"ctx": ynb}] + [{"tp": (z + d) % tp} for d in range(1, tp)])
+    line = LineGather(lout, lu, ld, lr)
 
     started = []
 
@@ -223,7 +559,7 @@
 
     acc[...] = jnp.zeros_like(acc)
     bsum[...] = jnp.zeros_like(bsum)
-    w_out[...] = w[0, :, 3 * mixed.shape[2] : 4 * mixed.shape[2]]
+    w_out[...] = w0[:, 3 * mixed.shape[2] : 4 * mixed.shape[2]]
 
     def project(b, r0, n):
         return dot_nt(mixed[b, pl.ds(r0, n), :], w_out[...])
@@ -258,8 +594,8 @@
 
     def mlp_forward(b, r0, n):
         rows_in = full[0, b, pl.ds(r0, n), :]
-        fa[pl.ds(0, n), :] = dot(rows_in, w[1])
-        fb[pl.ds(0, n), :] = dot(rows_in, w[2])
+        fa[pl.ds(0, n), :] = dot(rows_in, w[0])
+        fb[pl.ds(0, n), :] = dot(rows_in, w[1])
 
         def units(rows):
             g = fa[rows, :] + vec[6:7, :]
@@ -273,10 +609,10 @@
             hid[b, out, :] = (gelu * u).astype(BF16)
 
         tiles(0, n, units)
-        return dot_nt(hid[b, pl.ds(r0, n), :], w[3])
+        return dot_nt(hid[b, pl.ds(r0, n), :], w[2])
 
     def mlp_backward(b, r0, n):
-        fa[pl.ds(0, n), :] = dot(full[1, b, pl.ds(r0, n), :], w[3])
+        fa[pl.ds(0, n), :] = dot(full[1, b, pl.ds(r0, n), :], w[2])
 
         def units(rows):
             dh = fa[rows, :]
@@ -289,7 +625,7 @@
             bsum[1] += fold(du.astype(F32))
 
         tiles(0, n, units)
-        return dot_nt(dgt[b, pl.ds(r0, n), :], w[1]) + dot_nt(dup[b, pl.ds(r0, n), :], w[2])
+        return dot_nt(dgt[b, pl.ds(r0, n), :], w[0]) + dot_nt(dup[b, pl.ds(r0, n), :], w[1])
 
     def exchange(o, piece):
         own[...] = piece(c, 0, rows_own)
@@ -315,7 +651,7 @@
         center = res - jnp.mean(res, axis=-1, keepdims=True)
         r = lax.rsqrt(jnp.mean(center * center, axis=-1, keepdims=True) + 1e-12)
         zh = center * r
-        lout[rows, :] = (zh * vec[1:2, :] + vec[3:4, :]).astype(BF16)
+        lout[z, rows, :] = (zh * vec[1:2, :] + vec[3:4, :]).astype(BF16)
         up = cot[rows, :].astype(F32)
         t = up * vec[1:2, :]
         d = r * (t - jnp.mean(t, axis=-1, keepdims=True)
@@ -332,7 +668,9 @@
         tiles(k * cr, cr, norm_two)
         gather_start(1, k)
 
+    line.hop(0)
     exchange(2, mlp_backward)
+    line.hop(1)
 
     def flat(ref):
         return ref[...].reshape(4 * rows_own, ref.shape[-1])
@@ -343,6 +681,8 @@
     n_all = full[0].reshape(4 * rows_own, width)
     grads[0] = dot_tn(n_all, flat(dgt)).astype(BF16)
     grads[1] = dot_tn(n_all, flat(dup)).astype(BF16)
+
+    line.hop(2)
 
     def norm_back(rows):
         dn = summed(2, rows) + dres2[rows, :]
@@ -392,6 +732,8 @@
         ag_f[2, k].wait_recv()
         dmixed[dia, chunk(k), :] = unproject(dia, k * cr, cr)
     gout[...] = dot_tn(full[2].reshape(4 * rows_own, width), flat(mixed)).astype(BF16)
+    line.hop(3)
+    line.drain()
     for copy in started:
         copy.wait_send()
 
@@ -422,54 +764,92 @@
     units = geglu_weight.shape[2]
     assert units == width and 4 * cols == width and H == heads * tp
 
+    fused = shards == 2 and part_rows % 16 == 0
     with jax.named_scope("pack_weights"):
         first = jnp.concatenate(
             [qkv_weight[0], qkv_weight[1], qkv_weight[2], out_weight.T], axis=1
         )
-        parts = jnp.concatenate(
-            [first[None], geglu_weight, down_weight.T[None]], axis=0
-        )
-        own_bias = jnp.concatenate([qv_bias.reshape(1, -1), geglu_bias.reshape(1, -1)], axis=1)
         own_norm = jnp.concatenate([norm_gains, norm_biases, out_biases], axis=0)
-
-    with jax.named_scope("gather_weights"):
-        by_block = lax.all_gather(parts, "tp", axis=0)
-        swapped = lax.all_to_all(by_block, "ctx", split_axis=0, concat_axis=0)
-        w = lax.all_gather(swapped, "shard", axis=0)
-        w = w.transpose(2, 0, 1, 3, 4).reshape(4, shards * group * part_rows, width)
-        biases = lax.all_gather(own_bias, "tp", axis=0, tiled=True)
-        biases = lax.dynamic_slice_in_dim(biases, c, 1, 0).astype(F32)
-        norms = lax.all_gather(own_norm, ("shard", "ctx"), axis=1, tiled=True).astype(F32)
-    qv = biases[:, : 2 * cols].reshape(2, cols)
-    vec = jnp.concatenate([norms, biases[:, 2 * cols :].reshape(2, units)], axis=0)
+        me = lax.axis_index("shard") * group + c
+        if fused:
+            extra = jnp.zeros((16, width), BF16)
+            extra = extra.at[0, : 2 * cols].set(qv_bias.reshape(-1))
+            extra = extra.at[1:3].set(geglu_bias)
+            extra = lax.dynamic_update_slice(extra, own_norm, (3, me * part_rows))
+            p0 = jnp.concatenate([first, extra], axis=0)
+            pr = jnp.concatenate([geglu_weight, down_weight.T[None]], axis=0)
+        else:
+            parts = jnp.concatenate(
+                [first[None], geglu_weight, down_weight.T[None]], axis=0
+            )
+            own_bias = jnp.concatenate(
+                [qv_bias.reshape(1, -1), geglu_bias.reshape(1, -1)], axis=1)
 
     x_own = lax.dynamic_index_in_dim(tokens_in, z, 0, keepdims=False)
     cot_own = lax.dynamic_index_in_dim(cotangent, z, 0, keepdims=False)
     lengths = lax.dynamic_slice_in_dim(doc_lengths, z, 1, 0)
-    xs = lax.all_gather(x_own, "ctx", axis=0, tiled=True)
+    dma = lambda *shape: pltpu.SemaphoreType.DMA(shape)
     slopes = jnp.asarray([alibi_slopes(H)], F32)
-
     head_shape = sds((heads, length, DH), BF16)
-    mixed, probs, q, k, v = pl.pallas_call(
-        functools.partial(attention_forward, heads),
-        out_shape=[sds((length, cols), BF16), sds((heads, length, length), BF16)] + [head_shape] * 3,
-        in_specs=[smem(), smem()] + vmem(3),
-        out_specs=vmem(5),
-        scratch_shapes=[pltpu.VMEM((256, length), F32)],
-        compiler_params=pltpu.CompilerParams(vmem_limit_bytes=48 * MB),
-        name="attention_forward",
-    )(lengths, slopes, xs, w[0], qv)
+    if fused:
+        wide = part_rows + 16
+        stack4 = lambda n, r: pltpu.VMEM((n, r, width), BF16)
+        xs, w0, w, vec, mixed, probs, q, k, v = pl.pallas_call(
+            functools.partial(front, heads),
+            out_shape=[
+                sds((group, rows, width), BF16), sds((width, width), BF16),
+                sds((3, 2, group, part_rows, width), BF16), sds((8, width), F32),
+                sds((length, cols), BF16), sds((heads, length, length), BF16),
+            ] + [head_shape] * 3,
+            in_specs=[smem(), smem()] + vmem(3),
+            out_specs=vmem(9),
+            scratch_shapes=[
+                pltpu.VMEM((tp, wide, width), BF16), pltpu.VMEM((3, tp, part_rows, width), BF16),
+                pltpu.VMEM((2, group, wide, width), BF16), pltpu.VMEM((2, cols), F32),
+                pltpu.VMEM((rows, length), F32),
+                dma(3), dma(3), dma(4, 3), dma(4, 4), dma(4, 3), dma(4, 4), dma(4, 4), dma(4, 4),
+            ],
+            compiler_params=pltpu.CompilerParams(
+                collective_id=1, has_side_effects=True, vmem_limit_bytes=56 * MB
+            ),
+            name="front",
+        )(lengths, slopes, x_own, p0, pr)
+        w = w.reshape(3, width, width)
+    else:
+        with jax.named_scope("gather_weights"):
+            by_block = lax.all_gather(parts, "tp", axis=0)
+            swapped = lax.all_to_all(by_block, "ctx", split_axis=0, concat_axis=0)
+            w = lax.all_gather(swapped, "shard", axis=0)
+            w = w.transpose(2, 0, 1, 3, 4).reshape(4, shards * group * part_rows, width)
+            biases = lax.all_gather(own_bias, "tp", axis=0, tiled=True)
+            biases = lax.dynamic_slice_in_dim(biases, c, 1, 0).astype(F32)
+            norms = lax.all_gather(own_norm, ("shard", "ctx"), axis=1, tiled=True).astype(F32)
+        qv = biases[:, : 2 * cols].reshape(2, cols)
+        vec = jnp.concatenate([norms, biases[:, 2 * cols :].reshape(2, units)], axis=0)
+
+        xs = lax.all_gather(x_own, "ctx", axis=0, tiled=True)
+
+        mixed, probs, q, k, v = pl.pallas_call(
+            functools.partial(attention_forward, heads),
+            out_shape=[sds((length, cols), BF16), sds((heads, length, length), BF16)] + [head_shape] * 3,
+            in_specs=[smem(), smem()] + vmem(3),
+            out_specs=vmem(5),
+            scratch_shapes=[pltpu.VMEM((256, length), F32)],
+            compiler_params=pltpu.CompilerParams(vmem_limit_bytes=48 * MB),
+            name="attention_forward",
+        )(lengths, slopes, xs, w[0], qv)
+        w0, w = w[0], w[1:]
+
 
     block = (rows, width)
     stack = (group, rows, width)
-    dma = lambda *shape: pltpu.SemaphoreType.DMA(shape)
     lout, dres1, grads, gout, dmixed, small = pl.pallas_call(
         middle,
         out_shape=[
-            sds(block, BF16), sds(block, F32), sds((3, width, width), BF16),
+            sds((tp,) + block, BF16), sds(block, F32), sds((3, width, width), BF16),
             sds((width, cols), BF16), sds((group, rows, cols), BF16), sds((8, width), F32),
         ],
-        in_specs=vmem(5),
+        in_specs=vmem(6),
         out_specs=vmem(6),
         scratch_shapes=[
             pltpu.VMEM((width, cols), BF16), pltpu.VMEM((3,) + stack, BF16),
@@ -479,57 +859,92 @@
             pltpu.VMEM((rows, 1), F32), pltpu.VMEM(block, F32),
             pltpu.VMEM((6, 8, width), F32), pltpu.VMEM((2, 8, width), F32),
             pltpu.VMEM((4, 8, width), F32),
-        ] + [dma(3, NCH)] * 12 + [dma(2)] * 2,
+        ] + [dma(3, NCH)] * 12 + [dma(2)] * 2 + [dma(tp)] * 3,
         compiler_params=pltpu.CompilerParams(
             collective_id=0, has_side_effects=True, vmem_limit_bytes=58 * MB
         ),
         name="middle",
-    )(x_own, cot_own, mixed.reshape(group, rows, cols), w, vec)
-
-    grad_w, d_in, bias_grad = pl.pallas_call(
-        functools.partial(attention_backward, heads),
-        out_shape=[
-            sds((width, 3 * cols), BF16), sds((length, width), BF16), sds((1, 3 * cols), F32)
-        ],
-        in_specs=vmem(8),
-        out_specs=vmem(3),
-        scratch_shapes=[
-            pltpu.VMEM((length, 3 * cols), BF16),
-            pltpu.VMEM((heads, DH, length), F32), pltpu.VMEM((heads, DH, length), F32),
-        ],
-        compiler_params=pltpu.CompilerParams(vmem_limit_bytes=48 * MB),
-        name="attention_backward",
-    )(dmixed.reshape(length, cols), mixed, probs, q, k, v, xs, w[0])
-
-    with jax.named_scope("outputs"):
-        input_sum = lax.psum_scatter(d_in, "ctx", scatter_dimension=0, tiled=True)
-        input_own = (input_sum.astype(F32) + dres1).astype(BF16)
-        input_grad = lax.all_gather(input_own, "tp", axis=0).astype(F32)
-        layer_out = lax.all_gather(lout, "tp", axis=0)
-
-    with jax.named_scope("scatter_grads"):
-        first_grad = jnp.concatenate([grad_w, gout], axis=1)
-        packed = jnp.concatenate([first_grad[None], grads], axis=0)
-        packed = packed.reshape(4, shards, group, part_rows, width).transpose(1, 2, 0, 3, 4)
-        mine = lax.psum_scatter(packed, "shard", scatter_dimension=0, tiled=False)
-        mine = lax.all_to_all(mine, "ctx", split_axis=0, concat_axis=0)
-        mine = lax.psum_scatter(mine, "tp", scatter_dimension=0, tiled=False)
-        mine = mine.astype(F32)
-        grad_qkv = jnp.stack([mine[0, :, i * cols : (i + 1) * cols] for i in range(3)])
-        grad_out = mine[0, :, 3 * cols :].T
-        grad_geglu = mine[1:3]
-        grad_down = mine[3].T
+    )(x_own, cot_own, mixed.reshape(group, rows, cols), w0, w, vec)
+
+    if fused:
+        vm = pltpu.VMEM
+        out0, outr, input_low = pl.pallas_call(
+            functools.partial(back, heads),
+            out_shape=[
+                sds((wide, width), F32), sds((3, part_rows, width), F32), sds((tp,) + block, BF16)
+            ],
+            in_specs=vmem(12),
+            out_specs=vmem(3),
+            scratch_shapes=[
+                vm((length, 3 * cols), BF16),
+                vm((heads, DH, length), F32), vm((heads, DH, length), F32),
+                vm((16, width), F32), vm((width, width), BF16), vm((2, group, wide, width), BF16),
+            ] + [vm((group, wide, width), BF16), vm((3, group, part_rows, width), BF16)] * 4
+            + [vm(block, BF16)] * 6 + [vm(block, F32)] * 2
+            + [dma(4, 4)] * 6 + [dma(NCH)] * 6 + [dma(tp)] * 3,
+            compiler_params=pltpu.CompilerParams(
+                collective_id=2, has_side_effects=True, vmem_limit_bytes=56 * MB
+            ),
+            name="back",
+        )(
+            dmixed.reshape(length, cols), mixed, probs, q, k, v, xs, w0,
+            grads.reshape(3, 2, group, part_rows, width), gout, small, dres1,
+        )
+        layer_out = lout
+        input_grad = input_low.astype(F32)
+        grad_qkv = jnp.stack([out0[:part_rows, i * cols : (i + 1) * cols] for i in range(3)])
+        grad_out = out0[:part_rows, 3 * cols :].T
+        grad_geglu = outr[0:2]
+        grad_down = outr[2].T
         col = jnp.concatenate(
-            [bias_grad[:, :cols], bias_grad[:, 2 * cols :], small[6:7], small[7:8]], axis=1
-        )
-        col = lax.psum_scatter(
-            jnp.zeros((group, col.shape[1]), F32) + jnp.where(
-                jnp.arange(group)[:, None] == c, col, 0.0),
-            "tp", scatter_dimension=0, tiled=True)
-        col = lax.psum(col, ("shard", "ctx"))
-        norm_grad = lax.psum(small[:6], ("shard", "tp"))
-        me = lax.axis_index("shard") * group + c
-        norm_grad = lax.dynamic_slice_in_dim(norm_grad, me * part_rows, part_rows, 1)
+            [out0[part_rows : part_rows + 1, : 2 * cols],
+             out0[part_rows + 1 : part_rows + 3].reshape(1, 2 * units)], axis=1)
+        norm_grad = lax.dynamic_slice_in_dim(
+            out0[part_rows + 3 : part_rows + 9], me * part_rows, part_rows, 1)
+    else:
+        grad_w, d_in, bias_grad = pl.pallas_call(
+            functools.partial(attention_backward, heads),
+            out_shape=[
+                sds((width, 3 * cols), BF16), sds((length, width), BF16), sds((1, 3 * cols), F32)
+            ],
+            in_specs=vmem(8),
+            out_specs=vmem(3),
+            scratch_shapes=[
+                pltpu.VMEM((length, 3 * cols), BF16),
+                pltpu.VMEM((heads, DH, length), F32), pltpu.VMEM((heads, DH, length), F32),
+            ],
+            compiler_params=pltpu.CompilerParams(vmem_limit_bytes=48 * MB),
+            name="attention_backward",
+        )(dmixed.reshape(length, cols), mixed, probs, q, k, v, xs, w0)
+
+        with jax.named_scope("outputs"):
+            input_sum = lax.psum_scatter(d_in, "ctx", scatter_dimension=0, tiled=True)
+            input_own = (input_sum.astype(F32) + dres1).astype(BF16)
+            input_grad = lax.all_gather(input_own, "tp", axis=0).astype(F32)
+            layer_out = lout
+
+        with jax.named_scope("scatter_grads"):
+            first_grad = jnp.concatenate([grad_w, gout], axis=1)
+            packed = jnp.concatenate([first_grad[None], grads], axis=0)
+            packed = packed.reshape(4, shards, group, part_rows, width).transpose(1, 2, 0, 3, 4)
+            mine = lax.psum_scatter(packed, "shard", scatter_dimension=0, tiled=False)
+            mine = lax.all_to_all(mine, "ctx", split_axis=0, concat_axis=0)
+            mine = lax.psum_scatter(mine, "tp", scatter_dimension=0, tiled=False)
+            mine = mine.astype(F32)
+            grad_qkv = jnp.stack([mine[0, :, i * cols : (i + 1) * cols] for i in range(3)])
+            grad_out = mine[0, :, 3 * cols :].T
+            grad_geglu = mine[1:3]
+            grad_down = mine[3].T
+            col = jnp.concatenate(
+                [bias_grad[:, :cols], bias_grad[:, 2 * cols :], small[6:7], small[7:8]], axis=1
+            )
+            col = lax.psum_scatter(
+                jnp.zeros((group, col.shape[1]), F32) + jnp.where(
+                    jnp.arange(group)[:, None] == c, col, 0.0),
+                "tp", scatter_dimension=0, tiled=True)
+            col = lax.psum(col, ("shard", "ctx"))
+            norm_grad = lax.psum(small[:6], ("shard", "tp"))
+            norm_grad = lax.dynamic_slice_in_dim(norm_grad, me * part_rows, part_rows, 1)
     return (
         layer_out,
         input_grad,

time: 518 us -> 302 us (0.58)
  waiting for transfers between devices: 207 us -> 0 us
  Pallas kernels: 103 us -> 278 us
  blocking collectives: 154 us -> 0 us
  between operations: 14.4 us -> 0.74 us
  other arithmetic: 16 us -> 5.98 us
  local copies, waits for them, and re-layouts: 22.9 us -> 15.9 us
    pallas_call x3, Pallas kernels: 103 us -> 278 us  [the longest x1 110 us: on_device(): pl.pallas_call(functools.partial(back, heads), out_shape=[sds((wide, widt...]
    all_gather x5 -> x0, waiting for transfers between devices: 104 us -> none  [the longest x1 53.3 us: on_device(): by_block = lax.all_gather(parts, 'tp', axis=0)]
    reduce_scatter x3 -> x0, waiting for transfers between devices: 103 us -> none  [the longest x1 60.4 us: on_device(): mine = lax.psum_scatter(packed, 'shard', scatter_dimension=0, tiled=False)]
    all_to_all x2 -> x0, blocking collectives: 66 us -> none  [the longest x1 33 us: on_device(): mine = lax.all_to_all(mine, 'ctx', split_axis=0, concat_axis=0)]
    psum x2 -> x0, blocking collectives: 46.9 us -> none  [the longest x1 34.1 us: on_device(): norm_grad = lax.psum(small[:6], ('shard', 'tp'))]
    all_gather x2 -> x0, blocking collectives: 22 us -> none  [the longest x1 13.1 us: on_device(): biases = lax.all_gather(own_bias, 'tp', axis=0, tiled=True)]
    unnamed x1 -> x0, blocking collectives: 19.2 us -> none
    unnamed x40 -> x11, local copies, waits for them, and re-layouts: 11.1 us -> 3.46 us
  transfers between devices with their start and end apart: 8 -> 0, of which waited for: 6 -> 0; matrix products, arithmetic and copies ran while one was open for 4% -> 0% of each run, Pallas kernels for 0% -> 0%
where the time goes in v2:
time: 302 us; the launch traced here: 301 us
  Pallas kernels  278 us (92%)
  local copies, waits for them, and re-layouts  15.9 us (5%)
  other arithmetic  5.98 us (2%)
    pallas_call x1, Pallas kernels, on_device(): pl.pallas_call(functools.partial(back, heads), out_shape=[sds((wide, widt...  110 us
    pallas_call x1, Pallas kernels, on_device(): pl.pallas_call(functools.partial(front, heads), out_shape=[sds((group, ro...  87.1 us
    pallas_call x1, Pallas kernels, on_device(): pl.pallas_call(middle, out_shape=[sds((tp,) + block, BF16), sds(block, F3...  81.7 us

profile of v2, /device:TPU:0, one launch (start us, length us, event | category | flops | bytes accessed | tf_op | source)
XLA Modules:
  0.0 301.0 jit_solution(3061026798189803223)
XLA Ops:
  0.6 0.0 copy-start
  0.7 0.7 copy-done
  1.3 0.5 constant_dynamic-slice_fusion.1.lengths
  1.8 0.8 reshape.95
  2.6 0.7 pad_maximum_fusion.3
  3.3 0.8 scatter.9
  4.2 0.3 dynamic_update_slice.3
  4.5 0.9 copy.24
  5.4 0.9 slice_bitcast_fusion.7
  6.3 0.8 pad_maximum_fusion.2.p0
  7.0 1.8 pad_maximum_fusion.pr
  8.9 2.0 dynamic-slice_bitcast_fusion
  10.9 87.1 %front.1 = (bf16[4,256,768]{2,1,0:T(8,128)(2,1)}, bf16[768,768]{1,0:T(8,128)(2,1)}, bf16[3,2,4,96,768]{4,3,2,1,0:T(8,128)(2,1)}, f32[8,768]{1,0:T(8,128)}, bf16[...) custom-call(s32[1,8]{1,0:T(1,128)} %constant_dynamic-slice_fusion.1., ...), custom_call_target="tpu_custom_call" | custom-call | tf_op jit(solution)/shard_map/front/pallas_call | solution.py:797
  98.1 81.7 %middle.1 = (bf16[4,256,768]{2,1,0:T(8,128)(2,1)}, f32[256,768]{1,0:T(8,128)}, bf16[3,768,768]{2,1,0:T(8,128)(2,1)}, bf16[768,192]{1,0:T(8,128)(2,1)}, bf16[4,256,192]{2,1,0:T(8,128)(2,1)}, /*index=5*/f32[8,768]{1,0:T(8,128)}) custom-call(bf16[256,768]{1,0:T(8,128)(2,1)} %get-tuple-element.93.x, bf16[256,768]{1,0:T(8,128)(2,1)} %get-tuple-element.92.cot, ...), custom_call_target="tpu_custom_call" | custom-call | tf_op jit(solution)/shard_map/middle/pallas_call | solution.py:846
  179.7 109.5 %back.1 = (f32[112,768]{1,0:T(8,128)}, f32[3,96,768]{2,1,0:T(8,128)}, bf16[4,256,768]{2,1,0:T(8,128)(2,1)}) custom-call(bf16[1024,192]{1,0:T(8,128)(2,1)} %bitcast.33, bf16[1024,192]{1,0:T(8,128)(2,1)} %get-tuple-element.53.mixed, bf16[3,1024,1024]{2,1,0:T(8,128)(2,1)} %get-tuple-element.59.probs, bf16[3,1024,64]{2,1,0:T(8,128)(2,1)} %get-tuple-element.60.q, ...), custom_call_target="tpu_custom_call" | custom-call | tf_op jit(solution)/shard_map/back/pallas_call | solution.py:871
  289.3 0.0 copy-start.3
  289.3 0.8 slice_reduce_fusion
  290.1 0.7 reshape.100
  290.8 1.3 slice.87
  292.1 0.8 slice.89
  292.9 0.1 constant_dynamic-slice_fusion
  293.0 0.6 fusion
  293.6 0.0 copy-start.2
  293.6 1.3 slice_bitcast_fusion.1
  294.9 0.7 copy.25
  295.6 0.7 pad_maximum_fusion.1
  296.3 0.0 copy-done.3
  296.3 0.7 slice_bitcast_fusion
  297.1 0.9 slice.86
  297.9 0.0 copy-done.2
  297.9 0.0 copy-start.1
  297.9 1.9 convert_element_type.3
  299.9 0.0 copy-done.1
  299.9 1.1 copy.29
  (1 shorter events, 0.0 us)
Async XLA Ops:
  0.6 0.7 copy-start
  289.3 7.0 %copy-start.3 = (f32[3,96,768]{2,1,0:T(8,128)S(1)}, f32[3,96,768]{2,1,0:T(8,128)}, u32[]{:S(2)}) copy-start(f32[3,96,768]{2,1,0:T(8,128)} %get-tuple-element.70) | copy-start | bytes 2654212
  293.6 4.4 %copy-start.2 = (bf16[4,256,768]{2,1,0:T(8,128)(2,1)S(1)}, bf16[4,256,768]{2,1,0:T(8,128)(2,1)}, u32[]{:S(2)}) copy-start(bf16[4,256,768]{2,1,0:T(8,128)(2,1)} %get-tuple-element.68) | copy-start | bytes 4718596
  297.9 1.9 copy-start.1
